TPU v7x, 32 devices: a whole 2x2x4 slice. The times are simulated.
32 devices in a mesh: dp: 16 (over z, y, x), mp: 2 (over core).
Axes of the slice: x: 2, y: 2, z: 4, core: 2. Of those that a mesh axis runs over, the one named last changes fastest.
Arguments:
- series: bfloat16 [896, 32, 336], P('mp', 'dp'), may hold values from -6 to 6
- groups: int32 [32], P('dp'), may hold values from 0 to 2
- counts: int32 [32], P('dp'), may hold values from 574 to 862, as said below
- cotangent: bfloat16 [896, 32, 512], P('mp', 'dp'), may hold values from -18 to 18
- embed_weight: float32 [3, 336, 512], replicated, may hold values from -0.3125 to 0.3125
- embed_moment: float32 [3, 336, 512], replicated, may hold values from -6 to 6
- embed_error: float32 [16, 3, 336, 512], P('dp'), may hold values from -80 to 80
- embed_start: float32 [512, 8], replicated, may hold values from -6 to 6
- attend_weight: float32 [512, 3, 512], P(None, None, 'mp'), may hold values from -0.25 to 0.25
- attend_moment: float32 [512, 3, 512], P(None, None, 'mp'), may hold values from -6 to 6
- attend_error: float32 [16, 512, 3, 512], P('dp', None, None, 'mp'), may hold values from -80 to 80
- attend_start: float32 [3, 512, 8], P(None, 'mp'), may hold values from -6 to 6
- mixer_weight: float32 [512, 512], P('mp'), may hold values from -2 to 2
- mixer_moment: float32 [512, 512], P('mp'), may hold values from -6 to 6
- mixer_error: float32 [16, 512, 512], P('dp', 'mp'), may hold values from -80 to 80
- mixer_start: float32 [2, 512, 8], P('mp'), may hold values from -6 to 6
- inner_weight: float32 [512, 2048], P(None, 'mp'), may hold values from -0.25 to 0.25
- inner_moment: float32 [512, 2048], P(None, 'mp'), may hold values from -6 to 6
- inner_error: float32 [16, 512, 2048], P('dp', None, 'mp'), may hold values from -80 to 80
- inner_start: float32 [2048, 8], P('mp'), may hold values from -6 to 6
- outer_weight: float32 [2048, 512], P('mp'), may hold values from -0.125 to 0.125
- outer_moment: float32 [2048, 512], P('mp'), may hold values from -6 to 6
- outer_error: float32 [16, 2048, 512], P('dp', 'mp'), may hold values from -80 to 80
- outer_start: float32 [2, 512, 8], P('mp'), may hold values from -6 to 6
- embed_bias: float32 [3, 512], replicated, may hold values from -1.75 to 1.75
- embed_bias_moment: float32 [3, 512], replicated, may hold values from -6 to 6
- query_bias: float32 [2, 512], P(None, 'mp'), may hold values from -1.75 to 1.75
- query_bias_moment: float32 [2, 512], P(None, 'mp'), may hold values from -6 to 6
- inner_bias: float32 [2048], P('mp'), may hold values from -1.75 to 1.75
- inner_bias_moment: float32 [2048], P('mp'), may hold values from -6 to 6
- norm_gains: float32 [2, 512], replicated, may hold values from 0.5 to 1.5
- gains_moment: float32 [2, 512], replicated, may hold values from -6 to 6
- shared_biases: float32 [4, 512], replicated, may hold values from -1.75 to 1.75
- biases_moment: float32 [4, 512], replicated, may hold values from -6 to 6
Outputs:
- output: float32 [896, 32, 512], P('mp', 'dp')
- series_grad: float32 [896, 32, 336], P('mp', 'dp')
- embed_weight_new: float32 [3, 336, 512], replicated
- embed_moment_new: float32 [3, 336, 512], replicated
- embed_error_new: float32 [16, 3, 336, 512], P('dp')
- embed_left: float32 [3, 336, 8], replicated
- embed_right: float32 [512, 8], replicated
- attend_weight_new: float32 [512, 3, 512], P(None, None, 'mp')
- attend_moment_new: float32 [512, 3, 512], P(None, None, 'mp')
- attend_error_new: float32 [16, 512, 3, 512], P('dp', None, None, 'mp')
- attend_left: float32 [2, 512, 8], P('mp')
- attend_right: float32 [3, 512, 8], P(None, 'mp')
- mixer_weight_new: float32 [512, 512], P('mp')
- mixer_moment_new: float32 [512, 512], P('mp')
- mixer_error_new: float32 [16, 512, 512], P('dp', 'mp')
- mixer_left: float32 [512, 8], P('mp')
- mixer_right: float32 [2, 512, 8], P('mp')
- inner_weight_new: float32 [512, 2048], P(None, 'mp')
- inner_moment_new: float32 [512, 2048], P(None, 'mp')
- inner_error_new: float32 [16, 512, 2048], P('dp', None, 'mp')
- inner_left: float32 [2, 512, 8], P('mp')
- inner_right: float32 [2048, 8], P('mp')
- outer_weight_new: float32 [2048, 512], P('mp')
- outer_moment_new: float32 [2048, 512], P('mp')
- outer_error_new: float32 [16, 2048, 512], P('dp', 'mp')
- outer_left: float32 [2048, 8], P('mp')
- outer_right: float32 [2, 512, 8], P('mp')
- embed_bias_moment_new: float32 [3, 512], replicated
- embed_bias_new: float32 [3, 512], replicated
- query_bias_moment_new: float32 [2, 512], P(None, 'mp')
- query_bias_new: float32 [2, 512], P(None, 'mp')
- inner_bias_moment_new: float32 [2048], P('mp')
- inner_bias_new: float32 [2048], P('mp')
- gains_moment_new: float32 [2, 512], replicated
- norm_gains_new: float32 [2, 512], replicated
- biases_moment_new: float32 [4, 512], replicated
- shared_biases_new: float32 [4, 512], replicated
Inputs may be any that keep to these rules, and one draw needn't show every extreme that they name: `counts`: some window has exactly 862 live variates.
All inputs are finite; a program needn't handle non-finite values.
Results may differ from a plain program's by a relative error of at most 0.02.
Values may be sent and summed in bfloat16 or wider, within the bound.
A program may use at most 256 MiB of HBM per device.

v0:
```python
import functools
import math

import jax
import jax.numpy as jnp
from jax import lax
from jax.experimental import pallas as pl
from jax.experimental.pallas import tpu as pltpu
from jax.sharding import PartitionSpec as P

HEADS = 8
momentum_decay = 0.9
norm_epsilon = 1e-05
base_rate = 0.03
inverse_root_two = 0.7071067811865476
inverse_root_tau = 0.3989422804014327
log2_e = 1.4426950408889634
ln_two = 0.6931471805599453
f32 = jnp.float32
bf16 = jnp.bfloat16
VMEM = pltpu.VMEM
VM = pl.BlockSpec(memory_space=pltpu.VMEM)
HB = pl.BlockSpec(memory_space=pltpu.HBM)
MIB = 1024 * 1024


def dot_nn(a, b):
    return lax.dot_general(a, b, (((1,), (0,)), ((), ())), preferred_element_type=f32)


def dot_nt(a, b):
    return lax.dot_general(a, b, (((1,), (1,)), ((), ())), preferred_element_type=f32)


def dot_tn(a, b):
    return lax.dot_general(a, b, (((0,), (0,)), ((), ())), preferred_element_type=f32)


def split_two(x):
    high = x.astype(bf16)
    return high, (x - high.astype(f32)).astype(bf16)


def three_way(x, lane):
    high = x.astype(bf16).astype(f32)
    rest = x - high
    middle = rest.astype(bf16).astype(f32)
    last = rest - middle
    place = lax.rem(lax.rem(lane, 64), 3)
    return jnp.where(place == 0, high, jnp.where(place == 1, middle, last)).astype(bf16)


LIMITS = (12, 14, 12, 14, 16, 8, 8, 28)
TILES = 2


def row_number(rows, position):
    half = rows // 2
    index = lax.broadcasted_iota(jnp.int32, (rows, 128), 0)
    return jnp.where(index < half, index + position * half, index - half + (1 - position) * half)


def lookback_of(group, history):
    return jnp.where(
        group == 0, history * 2 // 7, jnp.where(group == 1, history * 4 // 7, history)
    ).astype(jnp.int32)


def take_window(pair_ref, window, home, columns):
    for index in range(2):

        @pl.when(window == index)
        def _(index=index):
            home[:, columns] = pair_ref[:, index, :]


def join_copies(mine, theirs, home, done):
    position = lax.axis_index("mp")
    return [
        pltpu.make_async_copy(source, home.at[:, window, :], done.at[index])
        for index, (source, window) in enumerate(((mine, position), (theirs, 1 - position)))
    ]


def three_parts(x):
    high = x.astype(bf16)
    rest = x - high.astype(f32)
    middle = rest.astype(bf16)
    return high, middle, (rest - middle.astype(f32)).astype(bf16)


def prepare(
    groups_hbm, counts_hbm, series_hbm, attend_hbm, query_bias_hbm, inner_bias_hbm,
    cot_hbm, mixer_hbm, inner_hbm, outer_hbm,
    send, received, series_own, small, facts, send_feed, cot_own,
    groups, counts, series, attend, query_bias, inner_bias, cotangent, mixer, inner, outer,
    done, send_sems, recv_sems,
):
    position = lax.axis_index("mp")
    partner = {"mp": 1 - position}
    barrier = pltpu.get_barrier_semaphore()
    pl.semaphore_signal(barrier, inc=1, device_id=partner, device_id_type=pl.DeviceIdType.MESH)
    copies = []
    for source, target in (
        (query_bias_hbm, query_bias), (inner_bias_hbm, inner_bias), (attend_hbm, attend),
        (series_hbm, series), (groups_hbm, groups), (counts_hbm, counts), (cot_hbm, cotangent),
        (mixer_hbm, mixer), (inner_hbm, inner), (outer_hbm, outer),
    ):
        copies.append(pltpu.make_async_copy(source, target, done.at[len(copies)]))
        copies[-1].start()
    half, _, history = series.shape
    width = send.shape[1]
    depth = attend.shape[1] // 2
    end = half + 3 * depth
    part = query_bias.shape[1]
    trades = [
        pltpu.make_async_remote_copy(
            src_ref=send.at[rows], dst_ref=received.at[rows], send_sem=send_sems.at[index],
            recv_sem=recv_sems.at[index], device_id=partner, device_id_type=pl.DeviceIdType.MESH,
        )
        for index, rows in enumerate((slice(half, end + 16), slice(0, half)))
    ]
    copies[0].wait()
    copies[1].wait()
    small[...] = jnp.zeros_like(small)
    small[0:2, :part] = query_bias[...]
    small[2:3, :] = inner_bias[...]
    values = jnp.concatenate(
        [
            jnp.concatenate([query_bias[0:1, :], query_bias[1:2, :]], axis=1),
            inner_bias[:, :width],
            inner_bias[:, width:],
            jnp.zeros((1, width), f32),
        ],
        axis=0,
    )
    send[end : end + 16, :] = jnp.concatenate(
        [*three_parts(values), jnp.zeros((4, width), bf16)], axis=0
    )
    copies[2].wait()
    for kind in range(3):
        rows = slice(half + kind * depth, half + (kind + 1) * depth)
        send[rows, :256] = attend[kind, :depth, :].astype(bf16)
        send[rows, 256:] = attend[kind, depth:, :].astype(bf16)
    pl.semaphore_wait(barrier, 1)
    trades[0].start()
    send[:half, 256:] = jnp.zeros((half, width - 256), bf16)
    copies[3].wait()
    take_window(series, 1 - position, send.at[:half], slice(0, history))
    trades[1].start()
    take_window(series, position, series_own, slice(None))
    copies[4].wait()
    copies[5].wait()
    group = jnp.where(position == 0, groups[0], groups[1])
    other_group = jnp.where(position == 0, groups[1], groups[0])
    count = jnp.where(position == 0, counts[0], counts[1])
    first = history - lookback_of(group, history)
    row = lax.broadcasted_iota(jnp.int32, facts.shape, 0)
    facts[...] = jnp.where(
        row == 0, count, jnp.where(row == 1, first, jnp.where(row == 2, group, other_group))
    )
    m, d, o = mixer.shape[0], inner.shape[0], outer.shape[0]
    copies[6].wait()
    take_window(cotangent, 1 - position, send_feed.at[m + 2 * d + o :], slice(None))
    take_window(cotangent, position, cot_own, slice(None))
    copies[7].wait()
    send_feed[:m] = mixer[...].astype(bf16)
    copies[8].wait()
    send_feed[m : m + d] = inner[:, :512].astype(bf16)
    send_feed[m + d : m + 2 * d] = inner[:, 512:].astype(bf16)
    copies[9].wait()
    send_feed[m + 2 * d : m + 2 * d + o] = outer[...].astype(bf16)
    for trade in trades:
        trade.wait()


def unpack_small(other, small_other):
    part = other.shape[1] // 2
    parts = other[other.shape[0] - 16 :, :].astype(f32)
    values = parts[0:4] + parts[4:8] + parts[8:12]
    small_other[0:1, :part] = values[0:1, :part]
    small_other[1:2, :part] = values[0:1, part:]
    small_other[2:3, : 2 * part] = values[1:2, :]
    small_other[2:3, 2 * part :] = values[2:3, :]


def attend_block(pack, half, kind):
    start = half + kind * 256
    return jnp.concatenate([pack[start : start + 256, :256], pack[start : start + 256, 256:]], axis=0)


def attend_forward(
    facts, series_own, embed, embed_bias, own, other, small,
    hidden_ref, token_ref, query_ref, key_ref, value_ref, context_ref, lse_ref, small_other, table, peak_ref,
):
    unpack_small(other, small_other)
    chosen, bias_row = embed[0], embed_bias[0:1, :]
    for group in range(1, embed.shape[0]):
        here = facts[2:3, 0:1] == group
        chosen = jnp.where(here, embed[group], chosen)
        bias_row = jnp.where(here, embed_bias[group : group + 1, :], bias_row)
    row = lax.broadcasted_iota(jnp.int32, chosen.shape, 0)
    table[...] = jnp.where(row >= facts[1:2, 0:1], chosen, 0.0).astype(bf16)
    rows, width = hidden_ref.shape
    half, history = series_own.shape
    part = width // 2
    head_dim = width // HEADS
    position, count = lax.axis_index("mp"), facts[0:1, 0:1]
    for index, block in enumerate((series_own[...], other[:half, :history])):
        values = dot_nn(block, table[...]) + bias_row
        hidden_ref[pl.ds(index * half, half), :] = values
        token_ref[pl.ds(index * half, half), :] = values.astype(bf16)
    scale = head_dim**-0.5 * log2_e
    tokens = token_ref[...]
    for index, (pack, bias) in enumerate(((own, small), (other, small_other))):
        columns = pl.ds(index * part, part)
        query_ref[:, columns] = (
            (dot_nn(tokens, attend_block(pack, half, 0)) + bias[0:1, :part]) * scale
        ).astype(bf16)
        key_ref[:, columns] = dot_nn(tokens, attend_block(pack, half, 1)).astype(bf16)
        value_ref[:, columns] = (
            dot_nn(tokens, attend_block(pack, half, 2)) + bias[1:2, :part]
        ).astype(bf16)
    lane = lax.broadcasted_iota(jnp.int32, (rows, 128), 1)
    dead = row_number(rows, position) >= count
    last = lax.rem(lane, 64) == 63
    extra_query = jnp.where(last, 1.0, 0.0).astype(bf16)
    extra_key = jnp.where(last & dead, -1e30, 0.0).astype(bf16)
    ones = jnp.ones((rows, 128), bf16)

    chooser = head_chooser(width, head_dim, 1.0)

    def longest(ref):
        values = ref[...].astype(f32)
        return jnp.max(dot_nn((values * values).astype(bf16), chooser), axis=0, keepdims=True)

    bound = jnp.max(longest(query_ref) * longest(key_ref))
    peak_ref[...] = jnp.zeros_like(peak_ref)

    @pl.when(jnp.logical_not(bound < 3600.0))
    def _():
        block = 128
        block_lane = lane[:block]

        def one_head(head, carry):
            columns = pl.ds(pl.multiple_of(head // 2 * 128, 128), 128)
            side = lax.rem(head, 2)
            query = jnp.where((lane // head_dim) == side, query_ref[:, columns], extra_query)

            def one_block(index, peak):
                place = pl.ds(pl.multiple_of(index * block, block), block)
                keys = key_ref[place, columns]
                far = lax.broadcasted_iota(jnp.int32, (block, 128), 0) + index * block
                near = jnp.where(
                    far < half, far + position * half, far - half + (1 - position) * half
                )
                mask = jnp.where(
                    (lax.rem(block_lane, 64) == 63) & (near >= count), -1e30, 0.0
                ).astype(bf16)
                scores = dot_nt(jnp.where((block_lane // head_dim) == side, keys, mask), query)
                return jnp.maximum(peak, jnp.max(scores, axis=0, keepdims=True))

            peak_ref[pl.ds(head, 1), :] = lax.fori_loop(
                0, rows // block, one_block, jnp.full((1, rows), -1e30, f32)
            )
            return carry

        lax.fori_loop(0, HEADS, one_head, 0)

    spread = part_spreader(-1.0)
    extra_query = jnp.where(
        last, 1.0, dot_tn(jnp.concatenate(three_parts(peak_ref[...]), axis=0), spread)
    ).astype(bf16)
    extra_key = jnp.where(last & dead, -1e30, 0.0)

    def pair(index, carry):
        columns = pl.ds(pl.multiple_of(index * 128, 128), 128)
        queries = query_ref[:, columns]
        keys = key_ref[:, columns]
        values = value_ref[:, columns]
        found = []
        for side in range(2):
            mine = (lane >= head_dim) if side else (lane < head_dim)
            hot = lax.rem(lane, 64) // 3 == index * 2 + side
            scores = dot_nt(
                jnp.where(mine, keys, jnp.where(hot, 1.0, extra_key).astype(bf16)),
                jnp.where(mine, queries, extra_query),
            )
            soft = jnp.exp2(scores).astype(bf16)
            mixed = dot_tn(jnp.where(mine, values, ones), soft)
            top, bottom = mixed[:head_dim], mixed[head_dim:]
            wanted, total = (bottom, top) if side else (top, bottom)
            found.append(wanted / total)
            place = pl.ds(index * 2 + side, 1)
            lse_ref[place, :] = jnp.log2(total[0:1]) + peak_ref[place, :]
        context_ref[:, columns] = jnp.concatenate(found, axis=0).T.astype(bf16)
        return carry

    lax.fori_loop(0, width // 128, pair, 0)


def part_spreader(value):
    row = lax.broadcasted_iota(jnp.int32, (3 * HEADS, 128), 0)
    lane = lax.broadcasted_iota(jnp.int32, (3 * HEADS, 128), 1)
    head = lax.rem(row, HEADS)
    wanted = lane == jnp.where(lax.rem(head, 2) == 0, 64, 0) + 3 * head + row // HEADS
    return jnp.where(wanted, value, 0.0).astype(bf16)


def head_chooser(width, head_dim, value):
    head = lax.broadcasted_iota(jnp.int32, (width, 128), 0) // head_dim
    lane = lax.broadcasted_iota(jnp.int32, (width, 128), 1)
    wanted = (lax.rem(lane, 64) // 3 == head) & ((lane >= 64) == (lax.rem(head, 2) == 0))
    return jnp.where(wanted, value, 0.0).astype(bf16)


def norm_rows(values, gain, shift):
    centered = values - jnp.mean(values, axis=-1, keepdims=True)
    inverse = lax.rsqrt(jnp.mean(centered * centered, axis=-1, keepdims=True) + norm_epsilon)
    unit = centered * inverse
    return unit * gain + shift, unit, inverse


def norm_rows_back(upstream, unit, inverse, gain):
    scaled = upstream * gain
    return inverse * (
        scaled
        - jnp.mean(scaled, axis=-1, keepdims=True)
        - unit * jnp.mean(scaled * unit, axis=-1, keepdims=True)
    )


def feed_forward(
    tiles, facts, context_ref, hidden_ref, own, other, small, small_other, gains, biases, cot_own,
    output_ref, output_send, active_near, preact_near, normed_ref, feed_ref, attend_ref, resid_ref,
    context_grad_ref, delta_ref, sums_ref, inner_sum_ref, grads_send, slope_ref, active_far, preact_far,
):
    rows, width = hidden_ref.shape
    tile = rows // tiles
    half = rows // 2
    part = width // 2
    inner_part = active_near.shape[1]
    units = 2 * inner_part
    chunk = 512
    position, count = lax.axis_index("mp"), facts[0:1, 0:1]
    sums_ref[...] = jnp.zeros_like(sums_ref)
    inner_sum_ref[...] = jnp.zeros_like(inner_sum_ref)
    at_inner = part
    at_outer = part + inner_part
    at_cot = at_outer + inner_part

    def inner_chunk(index):
        pack = (own, other)[index * chunk // inner_part]
        start = at_inner + (index * chunk % inner_part) // chunk * width
        return pack[start : start + width, :]

    def outer_chunk(index):
        pack = (own, other)[index * chunk // inner_part]
        start = at_outer + index * chunk % inner_part
        return pack[start : start + chunk, :]

    head_dim = width // HEADS
    chooser = head_chooser(width, head_dim, -1.0)

    def add(row, values):
        sums_ref[row : row + 1, :] += jnp.sum(values, axis=0, keepdims=True)

    def one_tile(step, carry):
        place = pl.ds(pl.multiple_of(step * tile, tile), tile)
        context = context_ref[place, :]
        attended = dot_nn(context[:, :part], own[:part, :]) + dot_nn(
            context[:, part:], other[:part, :]
        )
        normed, unit_one, inverse_one = norm_rows(
            hidden_ref[place, :] + attended + biases[2:3, :], gains[0:1, :], biases[0:1, :]
        )
        normed_low = normed.astype(bf16)
        normed_ref[place, :] = normed_low
        for index in range(units // chunk):
            columns = slice(index * chunk, (index + 1) * chunk)
            bias = (small, small_other)[index * chunk // inner_part]
            start = index * chunk % inner_part
            preact = dot_nn(normed_low, inner_chunk(index)) + bias[2:3, start : start + chunk]
            phi = 0.5 + 0.5 * lax.erf(preact * inverse_root_two)
            (active_near, active_far)[index * chunk // inner_part][place, start : start + chunk] = (preact * phi).astype(bf16)
            slope_ref[:, columns] = (
                phi + preact * jnp.exp2(preact * preact * (-0.5 * log2_e)) * inverse_root_tau
            ).astype(bf16)
        feed_out = dot_nn(active_near[place, :], own[at_outer:at_cot, :]) + dot_nn(
            active_far[place, :], other[at_outer:at_cot, :]
        )
        output, unit_two, inverse_two = norm_rows(
            normed + feed_out + biases[3:4, :], gains[1:2, :], biases[1:2, :]
        )
        index = lax.broadcasted_iota(jnp.int32, (tile, width), 0)

        @pl.when(step < tiles // 2)
        def _():
            output_ref[place, :] = output
        far = step - tiles // 2
        far_place = pl.ds(pl.multiple_of(jnp.maximum(far, 0) * tile, tile), tile)
        near_place = pl.ds(pl.multiple_of(jnp.minimum(step, tiles // 2 - 1) * tile, tile), tile)

        @pl.when(step >= tiles // 2)
        def _():
            output_send[far_place, :] = output
        cot = jnp.where(
            step < tiles // 2,
            cot_own[near_place, :],
            other[pl.ds(pl.multiple_of(at_cot + jnp.maximum(far, 0) * tile, 32), tile), :],
        ).astype(f32)
        first = jnp.where(
            step < tiles // 2,
            position * half + step * tile,
            (1 - position) * half + far * tile,
        )
        upstream = jnp.where(index + first < count, cot, 0.0)
        resid_two = norm_rows_back(upstream, unit_two, inverse_two, gains[1:2, :])
        feed_grad = resid_two.astype(bf16)
        feed_ref[place, :] = feed_grad
        for index in range(units // chunk):
            columns = slice(index * chunk, (index + 1) * chunk)
            grad = dot_nt(feed_grad, outer_chunk(index))
            start = index * chunk % inner_part
            (preact_near, preact_far)[index * chunk // inner_part][place, start : start + chunk] = (
                grad * slope_ref[:, columns].astype(f32)
            ).astype(bf16)
        normed_grad = resid_two
        for index in range(units // chunk):
            start = index * chunk % inner_part
            block = (preact_near, preact_far)[index * chunk // inner_part]
            normed_grad = normed_grad + dot_nt(
                block[place, start : start + chunk], inner_chunk(index)
            )
        resid_one = norm_rows_back(normed_grad, unit_one, inverse_one, gains[0:1, :])
        resid_ref[place, :] = resid_one
        attend_grad = resid_one.astype(bf16)
        attend_ref[place, :] = attend_grad
        context_grad = jnp.concatenate(
            [dot_nt(attend_grad, own[:part, :]), dot_nt(attend_grad, other[:part, :])], axis=1
        ).astype(bf16)
        context_grad_ref[place, :] = context_grad
        high, low = split_two(context_grad.astype(f32) * context.astype(f32))
        delta = dot_nn(high, chooser) + dot_nn(low, chooser)
        delta_ref[place, :] = three_way(delta, lax.broadcasted_iota(jnp.int32, (tile, 128), 1))
        add(1, normed_grad * unit_one)
        add(2, upstream * unit_two)
        add(3, normed_grad)
        add(4, upstream)
        add(5, resid_one)
        add(6, resid_two)
        for index, block in enumerate((preact_near, preact_far)):
            columns = slice(index * inner_part, (index + 1) * inner_part)
            inner_sum_ref[0:1, columns] += jnp.sum(
                block[place, :].astype(f32), axis=0, keepdims=True
            )
        return carry

    lax.fori_loop(0, tiles, one_tile, 0)
    grads_send[:inner_part, :] = dot_tn(active_far[...], feed_ref[...]).astype(bf16)
    for index in range(inner_part // chunk):
        start = index * chunk
        grads_send[inner_part + index * width : inner_part + (index + 1) * width, :] = dot_tn(
            normed_ref[...], preact_far[:, start : start + chunk]
        ).astype(bf16)
    grads_send[2 * inner_part :, :] = dot_tn(context_ref[:, part:], attend_ref[...]).astype(bf16)


def attend_backward(
    facts, query_ref, key_ref, value_ref, lse_ref, context_grad_ref, delta_ref,
    token_ref, resid_ref, own, other, table, series_own, sums_ref, inner_sum_ref,
    attend_own, send, series_near, series_far, near_out, far_out,
    dquery_ref, dkey_ref, dvalue_ref,
):
    rows, width = query_ref.shape
    head_dim = width // HEADS
    half, history = series_own.shape
    part = width // 2
    position, count = lax.axis_index("mp"), facts[0:1, 0:1]
    lane = lax.broadcasted_iota(jnp.int32, (rows, 128), 1)
    dead = row_number(rows, position) >= count
    last = lax.rem(lane, 64) == 63
    spread = part_spreader(-1.0)
    extra_query = jnp.where(
        last, 1.0, dot_tn(jnp.concatenate(three_parts(lse_ref[...]), axis=0), spread)
    ).astype(bf16)
    extra_key = jnp.where(last & dead, -1e30, 0.0)
    extra_grad = delta_ref[...]
    nothing = jnp.zeros((rows, 128), bf16)

    def pair(index, carry):
        columns = pl.ds(pl.multiple_of(index * 128, 128), 128)
        queries = query_ref[:, columns]
        keys = key_ref[:, columns]
        values = value_ref[:, columns]
        grads = context_grad_ref[:, columns]
        softs, score_grads, own_grads, own_queries, own_keys = [], [], [], [], []
        for side in range(2):
            mine = (lane >= head_dim) if side else (lane < head_dim)
            hot = lax.rem(lane, 64) // 3 == index * 2 + side
            soft = jnp.exp2(
                dot_nt(
                    jnp.where(mine, keys, jnp.where(hot, 1.0, extra_key).astype(bf16)),
                    jnp.where(mine, queries, extra_query),
                )
            )
            centered = dot_nt(
                jnp.where(mine, values, jnp.where(hot, 1.0, 0.0).astype(bf16)),
                jnp.where(mine, grads, extra_grad),
            )
            softs.append(soft.astype(bf16))
            score_grads.append((soft * centered).astype(bf16))
            own_grads.append(jnp.where(mine, grads, nothing))
            own_queries.append(jnp.where(mine, queries, nothing))
            own_keys.append(jnp.where(mine, keys, nothing))
        dvalue = dot_nn(jnp.concatenate(softs, axis=1), jnp.concatenate(own_grads, axis=0))
        dkey = dot_nn(jnp.concatenate(score_grads, axis=1), jnp.concatenate(own_queries, axis=0))
        dquery = dot_tn(jnp.concatenate(own_keys, axis=0), jnp.concatenate(score_grads, axis=0))
        dvalue_ref[:, columns] = dvalue.astype(bf16)
        dkey_ref[:, columns] = (dkey * ln_two).astype(bf16)
        dquery_ref[:, columns] = (dquery.T * head_dim**-0.5).astype(bf16)
        return carry

    lax.fori_loop(0, width // 128, pair, 0)

    tokens = token_ref[...]
    total = resid_ref[...]
    near_out[...] = jnp.zeros_like(near_out)
    far_out[...] = jnp.zeros_like(far_out)
    for kind, grad_ref in enumerate((dquery_ref, dkey_ref, dvalue_ref)):
        low = grad_ref[...]
        attend_own[kind] = dot_tn(tokens, low[:, :part])
        far = dot_tn(tokens, low[:, part:]).astype(bf16)
        send[kind * part : (kind + 1) * part, :part] = far[:part]
        send[kind * part : (kind + 1) * part, part:] = far[part:]
        total = (
            total
            + dot_nt(low[:, :part], attend_block(own, half, kind))
            + dot_nt(low[:, part:], attend_block(other, half, kind))
        )
        if kind != 1:
            column = jnp.sum(low.astype(f32), axis=0, keepdims=True)
            start = kind // 2 * part
            near_out[7:8, start : start + part] = column[:, :part]
            far_out[7:8, start : start + part] = column[:, part:]
    low = total.astype(bf16)
    series_near[...] = dot_nt(low[:half], table[...])
    series_far[...] = dot_nt(low[half:], table[...])
    table_grad = dot_tn(series_own[...], low[:half]) + dot_tn(other[:half, :history], low[half:])
    row = lax.broadcasted_iota(jnp.int32, table_grad.shape, 0)
    seen = row >= facts[1:2, 0:1]
    send[3 * part :, :] = jnp.where(seen, table_grad, 0.0).astype(bf16)
    shared = sums_ref[0:7, :]
    bias_grad = jnp.sum(low.astype(f32), axis=0, keepdims=True)
    near_out[0:7, :] = shared
    far_out[0:7, :] = shared
    near_out[0:1, :] = bias_grad
    far_out[0:1, :] = bias_grad
    count_near = inner_sum_ref.shape[1] // 2 // width
    for index in range(count_near):
        near_out[8 + index : 9 + index, :] = inner_sum_ref[0:1, index * width : (index + 1) * width]
        far_out[8 + index : 9 + index, :] = inner_sum_ref[
            0:1, (count_near + index) * width : (count_near + index + 1) * width
        ]


def left_product(start, matrix):
    both = dot_nt(jnp.concatenate(split_two(start), axis=0), matrix.astype(bf16))
    return both[:8] + both[8:]


def right_product(basis, matrix):
    both = dot_nn(jnp.concatenate(split_two(basis), axis=0), matrix.astype(bf16))
    return both[:8] + both[8:]


def feed_matrices(
    active_ref, preact_ref, normed_ref, feed_ref, context_ref, attend_ref, received,
    e_outer, e_inner, e_mixer, s_outer, s_inner, s_mixer, output_near, output_far,
    outer, inner, mixer, left, output, done,
):
    width = feed_ref.shape[1]
    inner_part = outer.shape[0]
    part = mixer.shape[0]
    chunk = 512
    copies = join_copies(output_near, output_far, output, done)
    for copy in copies:
        copy.start()
    outer[...] = (
        dot_tn(active_ref[...], feed_ref[...])
        + received[:inner_part, :].astype(f32)
        + e_outer[...]
    )
    for index in range(inner_part // chunk):
        columns = slice(index * chunk, (index + 1) * chunk)
        start = inner_part + index * width
        inner[:, columns] = (
            dot_tn(normed_ref[...], preact_ref[:, columns])
            + received[start : start + width, :].astype(f32)
            + e_inner[:, columns]
        )
    mixer[...] = (
        dot_tn(context_ref[:, :part], attend_ref[...])
        + received[2 * inner_part :, :].astype(f32)
        + e_mixer[...]
    )
    left[:, 0:1024] = left_product(s_outer[...], outer[...])
    left[:, 1024:1536] = left_product(s_inner[...], inner[...])
    left[:, 1536:1792] = left_product(s_mixer[...], mixer[...])
    for copy in copies:
        copy.wait()


def orthonormal_rows(blocks):
    rows = [lax.broadcasted_iota(jnp.int32, block.shape, 0) for block in blocks]
    for index in range(blocks[0].shape[0]):
        pivots = [block[index : index + 1, :] for block in blocks]
        inners = [jnp.sum(block * pivot, axis=1, keepdims=True) for block, pivot in zip(blocks, pivots)]
        sizes = [inner[index : index + 1, :] + 1e-12 for inner in inners]
        blocks = [
            jnp.where(
                row > index,
                block - pivot * (inner / size),
                jnp.where(row == index, block * lax.rsqrt(size), block),
            )
            for block, row, pivot, inner, size in zip(blocks, rows, pivots, inners, sizes)
        ]
    return blocks


def reduce_factors(
    replicas, facts, near_attend, own, received, e_attend, e_embed, s_attend, s_embed, left_part,
    near, far, outer, inner, mixer,
    left_ref, right_ref, mean_ref, attend, embed,
    start_ref, summed, partial, gathered, parts_one, parts_two, send_sems, recv_sems,
):
    me = lax.axis_index("dp")
    barrier = pltpu.get_barrier_semaphore()
    chunk = start_ref.shape[1] // replicas
    share = 1.0 / replicas

    paired = replicas & (replicas - 1) == 0

    def peer(offset):
        return jnp.bitwise_xor(me, offset) if paired else lax.rem(me + offset, replicas)

    def columns(index):
        return pl.ds(pl.multiple_of(index * chunk, 128), chunk)

    far_first = sorted(
        range(1, min(replicas, 17)), key=lambda k: -((k & 1) + (k >> 1 & 1) + (k >> 2))
    )

    def each(what):
        if replicas <= 16:
            for offset in far_first:
                what(offset)
            return

        def body(index, carry):
            what(replicas - index)
            return carry

        lax.fori_loop(1, replicas, body, 0)

    each(
        lambda offset: pl.semaphore_signal(
            barrier, inc=1, device_id={"dp": peer(offset)}, device_id_type=pl.DeviceIdType.MESH
        )
    )
    part = near_attend.shape[2]
    total = None
    for kind in range(3):
        rows = slice(kind * part, (kind + 1) * part)
        block = jnp.concatenate([received[rows, :part], received[rows, part:]], axis=0)
        attend[kind] = near_attend[kind] + block.astype(f32) + e_attend[kind]
        term = left_product(s_attend[kind], attend[kind])
        total = term if total is None else total + term
    mine, theirs = facts[2:3, 0:1], facts[3:4, 0:1]
    table_near = own[3 * part :, :].astype(f32)
    table_far = received[3 * part :, :].astype(f32)
    pieces = []
    for group in range(embed.shape[0]):
        grad = jnp.where(mine == group, table_near, 0.0) + jnp.where(theirs == group, table_far, 0.0)
        embed[group] = grad + e_embed[group]
        pieces.append(left_product(s_embed[...], embed[group]))
    used = embed.shape[0] * embed.shape[1]
    start_ref[:, 0:1024] = jnp.concatenate(pieces + [jnp.zeros((8, 1024 - used), f32)], axis=1)
    start_ref[:, 1024:2048] = left_part[:, 0:1024]
    start_ref[:, 2048:2560] = total
    start_ref[:, 2560:3328] = left_part[:, 1024:1792]
    common = near[1:7, :] + far[1:7, :]
    row = lax.broadcasted_iota(jnp.int32, (3, near.shape[1]), 0)
    bias = jnp.where(row == mine, near[0:1, :], 0.0) + jnp.where(row == theirs, far[0:1, :], 0.0)
    start_ref[:, 3328:3840] = jnp.concatenate([bias, common[:5]], axis=0)
    rest = jnp.concatenate([common[5:6], near[7:10, :] + far[7:10, :]], axis=0)
    for row in range(4):
        start_ref[2 * row : 2 * row + 1, 3840:4096] = rest[row : row + 1, :256]
        start_ref[2 * row + 1 : 2 * row + 2, 3840:4096] = rest[row : row + 1, 256:]
    if start_ref.shape[1] > 4096:
        start_ref[:, 4096:] = jnp.zeros((8, start_ref.shape[1] - 4096), f32)
    pl.semaphore_wait(barrier, replicas - 1)

    def all_sum(phase, source, parts, result):
        others = parts.at[pl.ds(1, replicas - 1)]

        def scatter(offset):
            other = peer(offset)
            return pltpu.make_async_remote_copy(
                src_ref=source.at[:, columns(other)],
                dst_ref=parts.at[offset],
                send_sem=send_sems.at[2 * phase],
                recv_sem=recv_sems.at[2 * phase],
                device_id={"dp": other},
                device_id_type=pl.DeviceIdType.MESH,
            )

        def spread(offset):
            return pltpu.make_async_remote_copy(
                src_ref=result.at[:, columns(me)],
                dst_ref=result.at[:, columns(me)],
                send_sem=send_sems.at[2 * phase + 1],
                recv_sem=recv_sems.at[2 * phase + 1],
                device_id={"dp": peer(offset)},
                device_id_type=pl.DeviceIdType.MESH,
            )

        def wait_all(semaphore):
            pltpu.make_async_copy(others, others, semaphore).wait()

        each(lambda offset: scatter(offset).start())
        wait_all(recv_sems.at[2 * phase])
        total = source[:, columns(me)]
        if replicas <= 16:
            for offset in range(1, replicas):
                total = total + parts[offset]
        else:
            total = lax.fori_loop(1, replicas, lambda offset, total: total + parts[offset], total)
        result[:, columns(me)] = total * share
        each(lambda offset: spread(offset).start())
        wait_all(recv_sems.at[2 * phase + 1])
        wait_all(send_sems.at[2 * phase])
        wait_all(send_sems.at[2 * phase + 1])

    all_sum(0, start_ref, parts_one, summed)
    mean_ref[...] = summed[:, 3328:4096]
    places = ((0, 1024), (1024, 1024), (2048, 512), (2560, 512), (3072, 256))
    bases = orthonormal_rows([summed[:, start : start + size] for start, size in places])
    for (start, size), basis in zip(places, bases):
        left_ref[:, start : start + size] = basis
    height = embed.shape[1]
    total = None
    for group in range(embed.shape[0]):
        term = right_product(bases[0][:, group * height : (group + 1) * height], embed[group])
        total = term if total is None else total + term
    partial[:, 0:512] = total
    partial[:, 512:1024] = right_product(bases[1], outer[...])
    for kind in range(3):
        partial[:, 1024 + kind * 256 : 1280 + kind * 256] = right_product(bases[2], attend[kind])
    partial[:, 1792:2816] = right_product(bases[3], inner[...])
    partial[:, 2816:3328] = right_product(bases[4], mixer[...])
    partial[:, 3328:] = jnp.zeros((8, partial.shape[1] - 3328), f32)
    all_sum(1, partial, parts_two, gathered)
    right_ref[...] = gathered[:, :3328]


def renew_all(
    step_rate, mixer_rate, left, right, mean, series_near, series_far, *refs,
):
    matrices, weights, moments = refs[0:5], refs[5:10], refs[10:15]
    vectors, vector_moments = refs[15:20], refs[20:25]
    errors, new_weights, new_moments = refs[25:30], refs[30:35], refs[35:40]
    new_vectors, new_vector_moments = refs[40:45], refs[45:50]
    lefts, rights, series_grad, done = refs[50:55], refs[55:60], refs[60], refs[61]
    step = pl.program_id(0)
    copies = join_copies(series_near, series_far, series_grad, done)

    @pl.when(step == 0)
    def _():
        for copy in copies:
            copy.start()

    def approx(basis, factor):
        left_high, left_low = split_two(basis)
        right_high, right_low = split_two(factor)
        return dot_tn(
            jnp.concatenate([left_high, left_low, left_high, left_low], axis=0),
            jnp.concatenate([right_high, right_high, right_low, right_low], axis=0),
        )

    def write(index, where, update, rate):
        errors[index][where] = matrices[index][where] - update
        moment = momentum_decay * moments[index][where] + update
        new_moments[index][where] = moment
        new_weights[index][where] = weights[index][where] - rate * moment

    def cut(start, size):
        return pl.ds(pl.multiple_of(start + step * size, 128), size)

    every = (slice(None), slice(None))
    groups, height, block = matrices[0].shape
    factor = right[:, cut(0, block)]
    for group in range(groups):
        write(
            0, (group, slice(None), slice(None)),
            approx(left[:, group * height : (group + 1) * height], factor), step_rate,
        )
    write(1, every, approx(left[:, cut(1024, matrices[1].shape[0])], right[:, 512:1024]), step_rate)
    basis = left[:, cut(2048, matrices[2].shape[1])]
    for kind in range(3):
        write(
            2, (kind, slice(None), slice(None)),
            approx(basis, right[:, 1024 + kind * 256 : 1280 + kind * 256]), step_rate,
        )
    write(3, every, approx(left[:, cut(2560, matrices[3].shape[0])], right[:, 1792:2816]), step_rate)
    write(4, every, approx(left[:, 3072:3328], right[:, cut(2816, matrices[4].shape[1])]), mixer_rate)

    @pl.when(step == 0)
    def _():
        for group in range(groups):
            lefts[0][group] = left[:, group * height : (group + 1) * height]
        lefts[1][...] = left[:, 1024:2048]
        lefts[2][...] = left[:, 2048:2560]
        lefts[3][...] = left[:, 2560:3072]
        lefts[4][...] = left[:, 3072:3328]
        rights[0][...] = right[:, 0:512]
        rights[1][...] = right[:, 512:1024]
        for kind in range(3):
            rights[2][kind] = right[:, 1024 + kind * 256 : 1280 + kind * 256]
        rights[3][...] = right[:, 1792:2816]
        rights[4][...] = right[:, 2816:3328]

        def renew(index, rows, columns, gradient):
            moment = momentum_decay * vector_moments[index][rows, columns] + gradient
            new_vector_moments[index][rows, columns] = moment
            new_vectors[index][rows, columns] = vectors[index][rows, columns] - step_rate * moment

        renew(0, slice(0, 3), slice(None), mean[0:3, :512])
        renew(1, slice(0, 2), slice(None), mean[3:5, :512])
        renew(2, slice(0, 3), slice(None), mean[5:8, :512])
        renew(2, slice(3, 4), slice(0, 256), mean[0:1, 512:])
        renew(2, slice(3, 4), slice(256, 512), mean[1:2, 512:])
        renew(3, slice(0, 1), slice(None), mean[2:3, 512:])
        renew(3, slice(1, 2), slice(None), mean[3:4, 512:])
        for index in range(4):
            renew(
                4, slice(0, 1), slice(index * 256, (index + 1) * 256),
                mean[4 + index : 5 + index, 512:],
            )

    @pl.when(step == pl.num_programs(0) - 1)
    def _():
        for copy in copies:
            copy.wait()


def call(
    kernel, outs, args, *, cost, in_specs=None, out_specs=None, scratch=(), limit=32, name=None
):
    return pl.pallas_call(
        kernel,
        out_shape=outs,
        in_specs=in_specs if in_specs is not None else [VM] * len(args),
        out_specs=out_specs if out_specs is not None else [VM] * len(outs),
        scratch_shapes=list(scratch),
        compiler_params=pltpu.CompilerParams(vmem_limit_bytes=limit * MIB),
        cost_estimate=estimate(cost),
        name=name,
    )(*args)


def estimate(microseconds):
    return pl.CostEstimate(
        flops=int(microseconds * 1e9), bytes_accessed=int(microseconds * 2e6), transcendentals=0
    )


def sds(shape, dtype=f32):
    return jax.ShapeDtypeStruct(shape, dtype)


def local(
    series, groups, counts, cotangent,
    embed_weight, embed_moment, embed_error, embed_start,
    attend_weight, attend_moment, attend_error, attend_start,
    mixer_weight, mixer_moment, mixer_error, mixer_start,
    inner_weight, inner_moment, inner_error, inner_start,
    outer_weight, outer_moment, outer_error, outer_start,
    embed_bias, embed_bias_moment, query_bias, query_bias_moment,
    inner_bias, inner_bias_moment, norm_gains, gains_moment, shared_biases, biases_moment,
):
    replicas = lax.axis_size("dp")
    half, windows, history = series.shape
    rows = 2 * half
    group_count, _, width = embed_weight.shape
    part = attend_weight.shape[2]
    inner_part = inner_weight.shape[1]
    units = 2 * inner_part
    turned = lambda a: a.transpose(1, 0, 2)

    def swap(values):
        return lax.ppermute(values, "mp", [(0, 1), (1, 0)])

    low = sds((rows, width), bf16)
    full = sds((rows, width))
    near = sds((half, width))
    packed = sds((half + 3 * part + 16, width), bf16)
    send_one, other_one, series_own, small, facts, send_two, cot_own = pl.pallas_call(
        prepare,
        out_shape=[
            packed, packed, sds((half, history), bf16), sds((8, inner_part)), sds((8, 128), jnp.int32),
            sds((part + 2 * inner_part + half, width), bf16), sds((half, width), bf16),
        ],
        in_specs=[HB] * 10,
        out_specs=[VM] * 7,
        scratch_shapes=[
            pltpu.SMEM(groups.shape, jnp.int32), pltpu.SMEM(counts.shape, jnp.int32),
            pltpu.VMEM(series.shape, bf16), pltpu.VMEM((3, width, part), f32),
            pltpu.VMEM(query_bias.shape, f32), pltpu.VMEM((1, inner_part), f32),
            pltpu.VMEM(cotangent.shape, bf16), pltpu.VMEM(mixer_weight.shape, f32),
            pltpu.VMEM(inner_weight.shape, f32), pltpu.VMEM(outer_weight.shape, f32),
            pltpu.SemaphoreType.DMA((10,)), pltpu.SemaphoreType.DMA((2,)), pltpu.SemaphoreType.DMA((2,)),
        ],
        compiler_params=pltpu.CompilerParams(
            collective_id=2, has_side_effects=True, vmem_limit_bytes=LIMITS[0] * MIB
        ),
        cost_estimate=estimate(7),
        name="prepare",
    )(
        *(
            pltpu.with_memory_space_constraint(a, pltpu.HBM)
            for a in (
                groups, counts, series, turned(attend_weight), query_bias, inner_bias[None],
                cotangent, mixer_weight, inner_weight, outer_weight,
            )
        )
    )
    other_two = swap(send_two)
    hidden, tokens, queries, keys, values, context, lse, small_other, table = call(
        attend_forward,
        [full, low, low, low, low, low, sds((HEADS, rows)), sds((8, inner_part)), sds((history, width), bf16)],
        (facts, series_own, embed_weight, embed_bias, send_one, other_one, small),
        limit=LIMITS[2], cost=15, scratch=[pltpu.VMEM((HEADS, rows), f32)],
        name="attend_forward",
    )
    (
        output_near, output_send, active, preact_grad, normed_low, feed_grad, attend_out, resid_one,
        context_grad, delta, sums, inner_sums, grads_send,
    ) = call(
        functools.partial(feed_forward, TILES),
        [near, near, sds((rows, inner_part), bf16), sds((rows, inner_part), bf16), low, low, low, full, low,
         sds((rows, 128), bf16), sds((8, width)), sds((8, units)),
         sds((2 * inner_part + part, width), bf16)],
        (facts, context, hidden, send_two, other_two, small, small_other, norm_gains, shared_biases, cot_own),
        limit=LIMITS[3], cost=22,
        scratch=[
            pltpu.VMEM((rows // TILES, units), bf16), pltpu.VMEM((rows, inner_part), bf16),
            pltpu.VMEM((rows, inner_part), bf16),
        ],
        name="feed_forward",
    )
    output_other = swap(output_send)
    grads_other = swap(grads_send)
    attend_near, send_three, series_near, series_far, sums_near, sums_far = call(
        attend_backward,
        [sds((3, width, part)), sds((3 * part + history, width), bf16), sds((half, history)),
         sds((half, history)), sds((16, width)), sds((16, width))],
        (facts, queries, keys, values, lse, context_grad, delta, tokens, resid_one, send_one,
         other_one, table, series_own, sums, inner_sums),
        limit=LIMITS[4], cost=22,
        scratch=[pltpu.VMEM((rows, width), bf16)] * 3,
        name="attend_backward",
    )
    other_three = swap(send_three)
    series_other = swap(series_far)
    sums_other = swap(sums_far)
    outer_matrix, inner_matrix, mixer_matrix, left_part, output = call(
        feed_matrices,
        [sds(outer_weight.shape), sds(inner_weight.shape), sds(mixer_weight.shape), sds((8, 1792)),
         sds((half, windows, width))],
        (active, preact_grad, normed_low, feed_grad, context, attend_out, grads_other,
         outer_error[0], inner_error[0], mixer_error[0], outer_start[0].T, inner_start.T, mixer_start[0].T,
         output_near, output_other),
        limit=LIMITS[5], cost=6, out_specs=[VM] * 4 + [HB],
        scratch=[pltpu.SemaphoreType.DMA((2,))],
        name="feed_matrices",
    )
    padded = max(128, -(-4096 // replicas // 128) * 128)
    total = padded * replicas
    left, right, mean, attend_matrix, embed_matrix = pl.pallas_call(
        functools.partial(reduce_factors, replicas),
        out_shape=[sds((8, 3328)), sds((8, 3328)), sds((8, 768)), sds((3, width, part)), sds(embed_weight.shape)],
        in_specs=[VM] * 14,
        out_specs=[VM] * 5,
        scratch_shapes=[
            pltpu.VMEM((8, total), f32), pltpu.VMEM((8, total), f32), pltpu.VMEM((8, total), f32),
            pltpu.VMEM((8, total), f32),
            pltpu.VMEM((replicas, 8, padded), f32), pltpu.VMEM((replicas, 8, padded), f32),
            pltpu.SemaphoreType.DMA((4,)), pltpu.SemaphoreType.DMA((4,)),
        ],
        compiler_params=pltpu.CompilerParams(
            collective_id=1, has_side_effects=True, vmem_limit_bytes=LIMITS[6] * MIB
        ),
        cost_estimate=estimate(30),
        name="reduce_factors",
    )(
        facts, attend_near, send_three, other_three, turned(attend_error[0]), embed_error[0],
        attend_start.transpose(0, 2, 1), embed_start.T, left_part, sums_near, sums_other,
        outer_matrix, inner_matrix, mixer_matrix,
    )
    matrices = (embed_matrix, outer_matrix, attend_matrix, inner_matrix, mixer_matrix)

    step_rate = base_rate * math.sqrt(replicas * 7 / (windows * rows))
    mixer_rate = step_rate * math.sqrt(width / max(width * 16 // rows, 1))
    steps = 4
    whole = lambda a: pl.BlockSpec(a.shape, lambda i: (0,) * len(a.shape))
    column = lambda a: pl.BlockSpec((a.shape[0], a.shape[1] // steps), lambda i: (0, i))
    row = lambda a: pl.BlockSpec((a.shape[0] // steps, a.shape[1]), lambda i: (i, 0))
    middle = lambda a: pl.BlockSpec((a.shape[0], a.shape[1] // steps, a.shape[2]), lambda i: (0, i, 0))
    last = lambda a: pl.BlockSpec((a.shape[0], a.shape[1], a.shape[2] // steps), lambda i: (0, 0, i))
    specs = [spec(a) for spec, a in zip((last, row, middle, row, column), matrices)]
    vectors = (embed_bias, norm_gains, shared_biases, query_bias, inner_bias[None])
    vector_moments = (
        embed_bias_moment, gains_moment, biases_moment, query_bias_moment, inner_bias_moment[None]
    )
    vector_specs = [whole(a) for a in vectors]
    factors = [
        sds((group_count, 8, history)), sds((8, 1024)), sds((8, 512)), sds((8, 512)), sds((8, 256)),
        sds((8, 512)), sds((8, 512)), sds((3, 8, part)), sds((8, 1024)), sds((8, 512)),
    ]
    found = pl.pallas_call(
        functools.partial(renew_all, step_rate, mixer_rate),
        grid=(steps,),
        out_shape=[sds(a.shape) for a in matrices] * 3 + [sds(a.shape) for a in vectors] * 2
        + factors + [sds(series.shape)],
        in_specs=[whole(left), whole(right), whole(mean), VM, VM] + specs * 3 + vector_specs * 2,
        out_specs=specs * 3 + vector_specs * 2 + [whole(a) for a in factors] + [HB],
        scratch_shapes=[pltpu.SemaphoreType.DMA((2,))],
        compiler_params=pltpu.CompilerParams(vmem_limit_bytes=LIMITS[7] * MIB),
        cost_estimate=estimate(12),
        name="renew_all",
    )(
        left, right, mean, series_near, series_other, *matrices,
        embed_weight, outer_weight, turned(attend_weight), inner_weight, mixer_weight,
        embed_moment, outer_moment, turned(attend_moment), inner_moment, mixer_moment,
        *vectors, *vector_moments,
    )
    errors, weights, moments = found[0:5], found[5:10], found[10:15]
    new_vectors, new_vector_moments = found[15:20], found[20:25]
    lefts, rights = found[25:30], found[30:35]
    return (
        output,
        found[35],
        weights[0],
        moments[0],
        errors[0][None],
        lefts[0].transpose(0, 2, 1),
        rights[0].T,
        turned(weights[2]),
        turned(moments[2]),
        turned(errors[2])[None],
        lefts[2].T[None],
        rights[2].transpose(0, 2, 1),
        weights[4],
        moments[4],
        errors[4][None],
        lefts[4].T,
        rights[4].T[None],
        weights[3],
        moments[3],
        errors[3][None],
        lefts[3].T[None],
        rights[3].T,
        weights[1],
        moments[1],
        errors[1][None],
        lefts[1].T,
        rights[1].T[None],
        new_vector_moments[0],
        new_vectors[0],
        new_vector_moments[3],
        new_vectors[3],
        new_vector_moments[4][0],
        new_vectors[4][0],
        new_vector_moments[1],
        new_vectors[1],
        new_vector_moments[2],
        new_vectors[2],
    )


def solution(mesh):
    return jax.shard_map(
        local,
        mesh=mesh,
        in_specs=(
            P("mp", "dp", None),
            P("dp"),
            P("dp"),
            P("mp", "dp", None),
            P(),
            P(),
            P("dp", None, None, None),
            P(),
            P(None, None, "mp"),
            P(None, None, "mp"),
            P("dp", None, None, "mp"),
            P(None, "mp", None),
            P("mp", None),
            P("mp", None),
            P("dp", "mp", None),
            P("mp", None, None),
            P(None, "mp"),
            P(None, "mp"),
            P("dp", None, "mp"),
            P("mp", None),
            P("mp", None),
            P("mp", None),
            P("dp", "mp", None),
            P("mp", None, None),
            P(),
            P(),
            P(None, "mp"),
            P(None, "mp"),
            P("mp"),
            P("mp"),
            P(),
            P(),
            P(),
            P(),
        ),
        out_specs=(
            P("mp", "dp", None),
            P("mp", "dp", None),
            P(),
            P(),
            P("dp", None, None, None),
            P(),
            P(),
            P(None, None, "mp"),
            P(None, None, "mp"),
            P("dp", None, None, "mp"),
            P("mp", None, None),
            P(None, "mp", None),
            P("mp", None),
            P("mp", None),
            P("dp", "mp", None),
            P("mp", None),
            P("mp", None, None),
            P(None, "mp"),
            P(None, "mp"),
            P("dp", None, "mp"),
            P("mp", None, None),
            P("mp", None),
            P("mp", None),
            P("mp", None),
            P("dp", "mp", None),
            P("mp", None),
            P("mp", None, None),
            P(),
            P(),
            P(None, "mp"),
            P(None, "mp"),
            P("mp"),
            P("mp"),
            P(),
            P(),
            P(),
            P(),
        ),
        check_vma=False,
    )
```

profile of v0, /device:TPU:0, one launch (start us, length us, event | category | flops | bytes accessed | tf_op | source)
XLA Modules:
  0.0 112.7 jit_solution(11392417240571562232)
XLA Ops:
  0.7 5.7 %prepare.1 = (bf16[1232,512]{1,0:T(8,128)(2,1)S(1)}, bf16[1232,512]{1,0:T(8,128)(2,1)S(1)}, bf16[448,336]{1,0:T(8,128)(2,1)S(1)}, f32[8,1024]{1,0:T(8,128)S(1)},...) custom-call(s32[2]{0:T(128)} %groups_hbm.1, s32[2]{0:T(128)} %counts_hbm.1, ...), custom_call_target="tpu_custom_call" | custom-call | flops 7000000000 | bytes 14000000 | tf_op jit(solution)/shard_map/prepare/pallas_call | solution.py:908
  6.4 0.5 collective-permute-start
  6.9 24.2 %attend_forward.1 = (f32[896,512]{1,0:T(8,128)S(1)}, bf16[896,512]{1,0:T(8,128)(2,1)S(1)}, bf16[896,512]{1,0:T(8,128)(2,1)S(1)}, bf16[896,512]{1,0:T(8,128)(2,1)...) custom-call(s32[8,128]{1,0:T(8,128)S(1)} %get-tuple-element.118.fact, ...), custom_call_target="tpu_custom_call" | custom-call | flops 15000000512 | bytes 30000000 | tf_op jit(solution)/shard_map/attend_forward/pallas_call | solution.py:860
  31.1 18.1 %feed_forward.1 = (f32[448,512]{1,0:T(8,128)S(1)}, f32[448,512]{1,0:T(8,128)S(1)}, bf16[896,1024]{1,0:T(8,128)(2,1)S(1)}, bf16[896,1024]{1,0:T(8,128)(2,1)S(1)},...) custom-call(s32[8,128]{1,0:T(8,128)S(1)} %get-tuple-element.118.fact, ...), custom_call_target="tpu_custom_call" | custom-call | flops 22000001024 | bytes 44000000 | tf_op jit(solution)/shard_map/feed_forward/pallas_call | solution.py:860
  49.3 0.1 collective-permute-start.2
  49.4 0.5 collective-permute-start.1
  49.9 0.0 copy-start.17
  49.9 21.3 %attend_backward.1 = (f32[3,512,256]{2,1,0:T(8,128)S(1)}, bf16[1104,512]{1,0:T(8,128)(2,1)S(1)}, f32[448,336]{1,0:T(8,128)S(1)}, f32[448,336]{1,0:T(8,128)S(1)},...) custom-call(s32[8,128]{1,0:T(8,128)S(1)} %get-tuple-element.118.facts, bf16[896,512]{1,0:T(8,128)(2,1)S(1)} %get-tuple-element.137.query_ref, ...), custom_call_target="tpu_custom_call" | custom-call | flops 22000001024 | bytes 44000000 | tf_op jit(solution)/shard_map/attend_backward/pallas_call | solution.py:860
  71.2 0.1 collective-permute-start.3
  71.3 0.4 collective-permute-start.4
  71.7 0.1 collective-permute-start.5
  71.9 0.0 copy-start.6
  71.9 0.0 copy-start.19
  71.9 3.4 %feed_matrices.1 = (f32[1024,512]{1,0:T(8,128)S(1)}, f32[512,1024]{1,0:T(8,128)S(1)}, f32[256,512]{1,0:T(8,128)S(1)}, f32[8,1792]{1,0:T(8,128)S(1)}, f32[448,2,512]{2,1,0:T(2,128)}) custom-call(bf16[896,1024]{1,0:T(8,128)(2,1)S(1)} %get-tuple-element.128.active_ref, bf16[896,1024]{1,0:T(8,128)(2,1)S(1)} %get-tuple-element.129.preact_ref, ...), custom_call_target="tpu_custom_call" | custom-call | flops 6000000000 | bytes 12000000 | tf_op jit(solution)/shard_map/feed_matrices/pallas_call | solution.py:860
  75.4 0.0 copy-start.2
  75.4 0.0 copy-start.5
  75.4 0.0 copy-start.8
  75.5 0.0 copy-start.13
  75.5 0.0 copy-start.14
  75.5 0.0 copy-start.24
  75.5 0.0 copy-start.26
  75.6 0.0 copy-start.29
  75.6 26.5 %reduce_factors.1 = (f32[8,3328]{1,0:T(8,128)S(1)}, f32[8,3328]{1,0:T(8,128)S(1)}, f32[8,768]{1,0:T(8,128)S(1)}, f32[3,512,256]{2,1,0:T(8,128)S(1)}, f32[3,336,512]{2,1,0:T(8,128)S(1)}) custom-call(s32[8,128]{1,0:T(8,128)S(1)} %get-tuple-element.118.facts, f32[3,512,256]{2,1,0:T(8,128)S(1)} %get-tuple-element.148.near_attend, ...), custom_call_target="tpu_custom_call" | custom-call | flops 30000001024 | bytes 60000000 | tf_op jit(solution)/shard_map/reduce_factors/pallas_call | solution.py:990
  102.2 10.3 %renew_all.1 = (f32[3,336,512]{2,1,0:T(8,128)}, f32[1024,512]{1,0:T(8,128)}, f32[3,512,256]{2,1,0:T(8,128)}, f32[512,1024]{1,0:T(8,128)}, f32[256,512]{1,0:T(8,1...) custom-call(f32[8,3328]{1,0:T(8,128)S(1)} %get-tuple-element.156.lef, ...), custom_call_target="tpu_custom_call" | custom-call | flops 12000000000 | bytes 24000000 | tf_op jit(solution)/shard_map/renew_all/pallas_call | solution.py:1031
  (55 shorter events, 0.1 us)
Async XLA Ops:
  6.4 24.7 %collective-permute-start = (bf16[2752,512]{1,0:T(8,128)(2,1)S(1)}, bf16[2752,512]{1,0:T(8,128)(2,1)S(1)}, u32[]{:S(2)}, u32[]{:S(2)}) collective-permute-start(bf16[2752,512]{1,0:T(8,128)(2,1)S(1)} %get-tuple-element.125.own), channel_id=1, source_target_pairs={{0,1},{1,0},{2,3},{3,2},{4,5},{5,4},{6,7},{7,6},{8,9},{9,8},{10,11... | collective-permute-start | bytes 8454152 | tf_op jit(solution)/shard_map/ppermute | solution.py:902
  6.9 24.2 %copy-start.21 = (f32[4,512]{1,0:T(4,128)S(1)}, f32[4,512]{1,0:T(4,128)}, u32[]{:S(2)}) copy-start(f32[4,512]{1,0:T(4,128)} %refs_17_.1) | copy-start | bytes 24580
  6.9 24.2 %copy-start.25 = (f32[2,512]{1,0:T(2,128)S(1)}, f32[2,512]{1,0:T(2,128)}, u32[]{:S(2)}) copy-start(f32[2,512]{1,0:T(2,128)} %refs_16_.1) | copy-start | bytes 12292
  49.3 22.5 %collective-permute-start.2 = (f32[448,512]{1,0:T(8,128)S(1)}, f32[448,512]{1,0:T(8,128)S(1)}, u32[]{:S(2)}, u32[]{:S(2)}) collective-permute-start(f32[448,512]{1,0:T(8,128)S(1)} %get-tuple-element.135), channel_id=1, source_target_pairs={{0,1},{1,0},{2,3},{3,2},{4,5},{5,4},{6,7},{7,6},{8,9},{9,8},{10,11... | collective-permute-start | bytes 2752520 | tf_op jit(solution)/shard_map/ppermute | solution.py:902
  49.4 22.5 %collective-permute-start.1 = (bf16[2304,512]{1,0:T(8,128)(2,1)S(1)}, bf16[2304,512]{1,0:T(8,128)(2,1)S(1)}, u32[]{:S(2)}, u32[]{:S(2)}) collective-permute-start(bf16[2304,512]{1,0:T(8,128)(2,1)S(1)} %get-tuple-element.133), channel_id=1, source_target_pairs={{0,1},{1,0},{2,3},{3,2},{4,5},{5,4},{6,7},{7,6},{8,9},{9,8},{10,11... | collective-permute-start | bytes 7077896 | tf_op jit(solution)/shard_map/ppermute | solution.py:902
  71.2 4.2 %collective-permute-start.3 = (bf16[1104,512]{1,0:T(8,128)(2,1)S(1)}, bf16[1104,512]{1,0:T(8,128)(2,1)S(1)}, u32[]{:S(2)}, u32[]{:S(2)}) collective-permute-start(bf16[1104,512]{1,0:T(8,128)(2,1)S(1)} %get-tuple-element.149.own), channel_id=1, source_target_pairs={{0,1},{1,0},{2,3},{3,2},{4,5},{5,4},{6,7},{7,6},{8,9},{9,8},{10,11... | collective-permute-start | bytes 3391496 | tf_op jit(solution)/shard_map/ppermute | solution.py:902
  71.3 4.0 %collective-permute-start.4 = (f32[16,512]{1,0:T(8,128)S(1)}, f32[16,512]{1,0:T(8,128)S(1)}, u32[]{:S(2)}, u32[]{:S(2)}) collective-permute-start(f32[16,512]{1,0:T(8,128)S(1)} %get-tuple-element.152), channel_id=1, source_target_pairs={{0,1},{1,0},{2,3},{3,2},{4,5},{5,4},{6,7},{7,6},{8,9},{9,8},{10,11... | collective-permute-start | bytes 98312 | tf_op jit(solution)/shard_map/ppermute | solution.py:902
  71.7 30.3 %collective-permute-start.5 = (f32[448,336]{1,0:T(8,128)S(1)}, f32[448,336]{1,0:T(8,128)S(1)}, u32[]{:S(2)}, u32[]{:S(2)}) collective-permute-start(f32[448,336]{1,0:T(8,128)S(1)} %get-tuple-element.160), channel_id=1, source_target_pairs={{0,1},{1,0},{2,3},{3,2},{4,5},{5,4},{6,7},{7,6},{8,9},{9,8},{10,11... | collective-permute-start | bytes 1806344 | tf_op jit(solution)/shard_map/ppermute | solution.py:902
  75.4 26.7 %copy-start.2 = (f32[512,1024]{1,0:T(8,128)S(1)}, f32[512,1024]{1,0:T(8,128)}, u32[]{:S(2)}) copy-start(f32[512,1024]{1,0:T(8,128)} %refs_8_.1) | copy-start | bytes 6291460
  75.4 26.7 %copy-start.3 = (f32[1024,512]{1,0:T(8,128)S(1)}, f32[1024,512]{1,0:T(8,128)}, u32[]{:S(2)}) copy-start(f32[1024,512]{1,0:T(8,128)} %refs_6_.1) | copy-start | bytes 6291460
  75.4 26.7 %copy-start.4 = (f32[1024,512]{1,0:T(8,128)S(1)}, f32[1024,512]{1,0:T(8,128)}, u32[]{:S(2)}) copy-start(f32[1024,512]{1,0:T(8,128)} %refs_11_.1) | copy-start | bytes 6291460
  75.4 26.7 %copy-start.5 = (f32[512,1024]{1,0:T(8,128)S(1)}, f32[512,1024]{1,0:T(8,128)}, u32[]{:S(2)}) copy-start(f32[512,1024]{1,0:T(8,128)} %refs_13_.1) | copy-start | bytes 6291460
  75.4 26.7 %copy-start.8 = (f32[3,336,512]{2,1,0:T(8,128)S(1)}, f32[3,336,512]{2,1,0:T(8,128)}, u32[]{:S(2)}) copy-start(f32[3,336,512]{2,1,0:T(8,128)} %refs_10_.1) | copy-start | bytes 6193156
  75.5 26.7 %copy-start.10 = (f32[512,3,256]{2,0,1:T(8,128)S(1)}, f32[512,3,256]{2,0,1:T(8,128)}, u32[]{:S(2)}) copy-start(f32[512,3,256]{2,0,1:T(8,128)} %param.42) | copy-start | bytes 4718596
  75.5 26.7 %copy-start.11 = (f32[512,3,256]{2,0,1:T(8,128)S(1)}, f32[512,3,256]{2,0,1:T(8,128)}, u32[]{:S(2)}) copy-start(f32[512,3,256]{2,0,1:T(8,128)} %param.43) | copy-start | bytes 4718596
  75.5 26.7 %copy-start.13 = (f32[256,512]{1,0:T(8,128)S(1)}, f32[256,512]{1,0:T(8,128)}, u32[]{:S(2)}) copy-start(f32[256,512]{1,0:T(8,128)} %refs_9_.1) | copy-start | bytes 1572868
  75.5 26.7 %copy-start.14 = (f32[256,512]{1,0:T(8,128)S(1)}, f32[256,512]{1,0:T(8,128)}, u32[]{:S(2)}) copy-start(f32[256,512]{1,0:T(8,128)} %refs_14_.1) | copy-start | bytes 1572868
  75.5 26.7 %copy-start.22 = (f32[3,512]{1,0:T(4,128)S(1)}, f32[3,512]{1,0:T(4,128)}, u32[]{:S(2)}) copy-start(f32[3,512]{1,0:T(4,128)} %refs_20_.1) | copy-start | bytes 18436
  75.5 26.7 %copy-start.23 = (f32[4,512]{1,0:T(4,128)S(1)}, f32[4,512]{1,0:T(4,128)}, u32[]{:S(2)}) copy-start(f32[4,512]{1,0:T(4,128)} %refs_22_.1) | copy-start | bytes 24580
  75.5 26.7 %copy-start.24 = (f32[1024]{0:T(1024)S(1)}, f32[1024]{0:T(1024)}, u32[]{:S(2)}) copy-start(f32[1024]{0:T(1024)} %param.62) | copy-start | bytes 12292
  75.5 26.7 %copy-start.26 = (f32[2,512]{1,0:T(2,128)S(1)}, f32[2,512]{1,0:T(2,128)}, u32[]{:S(2)}) copy-start(f32[2,512]{1,0:T(2,128)} %refs_21_.1) | copy-start | bytes 12292
  75.6 26.7 %copy-start.27 = (f32[1024]{0:T(1024)S(1)}, f32[1024]{0:T(1024)}, u32[]{:S(2)}) copy-start(f32[1024]{0:T(1024)} %param.63) | copy-start | bytes 12292
  75.6 26.7 %copy-start.28 = (f32[2,256]{1,0:T(2,128)S(1)}, f32[2,256]{1,0:T(2,128)}, u32[]{:S(2)}) copy-start(f32[2,256]{1,0:T(2,128)} %refs_18_.1) | copy-start | bytes 6148
  75.6 26.7 %copy-start.29 = (f32[2,256]{1,0:T(2,128)S(1)}, f32[2,256]{1,0:T(2,128)}, u32[]{:S(2)}) copy-start(f32[2,256]{1,0:T(2,128)} %refs_23_.1) | copy-start | bytes 6148
  (12 other events, 158.3 us)
where the time goes:
time: 113 us
  Pallas kernels  109 us (96%)
  starting transfers between devices  1.74 us (2%)
  between operations  1.37 us (1%)
    pallas_call x4, Pallas kernels, call(): pl.pallas_call(kernel, out_shape=outs, in_specs=in_specs if in_specs is n...  67 us
    pallas_call x1, Pallas kernels, local(): pl.pallas_call(functools.partial(reduce_factors, replicas), out_shape=[sd...  26.5 us
    pallas_call x1, Pallas kernels, local(): pl.pallas_call(functools.partial(renew_all, step_rate, mixer_rate), grid=...  10.3 us
    pallas_call x1, Pallas kernels, local(): pl.pallas_call(prepare, out_shape=[packed, packed, sds((half, history), b...  5.67 us
  transfers between devices with their start and end apart: 6, of which 0 were waited for; matrix products, arithmetic and copies ran while one was open for 0% of the time, Pallas kernels for 67%

commit v1 on v0

--- a/solution.py
+++ b/solution.py
@@ -50,7 +50,7 @@
     return jnp.where(place == 0, high, jnp.where(place == 1, middle, last)).astype(bf16)
 
 
-LIMITS = (12, 14, 12, 14, 16, 8, 8, 28)
+LIMITS = (12, 14, 12, 14, 16, 8, 8, 18)
 TILES = 2
 
 
@@ -107,7 +107,8 @@
         (mixer_hbm, mixer), (inner_hbm, inner), (outer_hbm, outer),
     ):
         copies.append(pltpu.make_async_copy(source, target, done.at[len(copies)]))
-        copies[-1].start()
+    for copy in copies[:6]:
+        copy.start()
     half, _, history = series.shape
     width = send.shape[1]
     depth = attend.shape[1] // 2
@@ -115,10 +116,15 @@
     part = query_bias.shape[1]
     trades = [
         pltpu.make_async_remote_copy(
-            src_ref=send.at[rows], dst_ref=received.at[rows], send_sem=send_sems.at[index],
+            src_ref=send.at[place], dst_ref=received.at[place], send_sem=send_sems.at[index],
             recv_sem=recv_sems.at[index], device_id=partner, device_id_type=pl.DeviceIdType.MESH,
         )
-        for index, rows in enumerate((slice(half, end + 16), slice(0, half)))
+        for index, place in enumerate(
+            (
+                (slice(half, end + 16), slice(None)),
+                (slice(0, half), slice(0, -(-history // 128) * 128)),
+            )
+        )
     ]
     copies[0].wait()
     copies[1].wait()
@@ -138,6 +144,8 @@
         [*three_parts(values), jnp.zeros((4, width), bf16)], axis=0
     )
     copies[2].wait()
+    for copy in copies[6:]:
+        copy.start()
     for kind in range(3):
         rows = slice(half + kind * depth, half + (kind + 1) * depth)
         send[rows, :256] = attend[kind, :depth, :].astype(bf16)
@@ -788,32 +796,46 @@
             jnp.concatenate([right_high, right_high, right_low, right_low], axis=0),
         )
 
-    def write(index, where, update, rate):
-        errors[index][where] = matrices[index][where] - update
-        moment = momentum_decay * moments[index][where] + update
+    def write(index, read, where, update, rate):
+        errors[index][where] = matrices[index][read] - update
+        moment = momentum_decay * moments[index][read] + update
         new_moments[index][where] = moment
-        new_weights[index][where] = weights[index][where] - rate * moment
+        new_weights[index][where] = weights[index][read] - rate * moment
 
     def cut(start, size):
         return pl.ds(pl.multiple_of(start + step * size, 128), size)
 
-    every = (slice(None), slice(None))
-    groups, height, block = matrices[0].shape
+    all_of = slice(None)
+    every = (all_of, all_of)
+    groups, height, block = errors[0].shape
     factor = right[:, cut(0, block)]
     for group in range(groups):
         write(
-            0, (group, slice(None), slice(None)),
+            0, (group, all_of, cut(0, block)), (group, all_of, all_of),
             approx(left[:, group * height : (group + 1) * height], factor), step_rate,
         )
-    write(1, every, approx(left[:, cut(1024, matrices[1].shape[0])], right[:, 512:1024]), step_rate)
-    basis = left[:, cut(2048, matrices[2].shape[1])]
+    block = errors[1].shape[0]
+    write(
+        1, (cut(0, block), all_of), every, approx(left[:, cut(1024, block)], right[:, 512:1024]),
+        step_rate,
+    )
+    block = errors[2].shape[1]
+    basis = left[:, cut(2048, block)]
     for kind in range(3):
         write(
-            2, (kind, slice(None), slice(None)),
+            2, (kind, cut(0, block), all_of), (kind, all_of, all_of),
             approx(basis, right[:, 1024 + kind * 256 : 1280 + kind * 256]), step_rate,
         )
-    write(3, every, approx(left[:, cut(2560, matrices[3].shape[0])], right[:, 1792:2816]), step_rate)
-    write(4, every, approx(left[:, 3072:3328], right[:, cut(2816, matrices[4].shape[1])]), mixer_rate)
+    block = errors[3].shape[0]
+    write(
+        3, (cut(0, block), all_of), every, approx(left[:, cut(2560, block)], right[:, 1792:2816]),
+        step_rate,
+    )
+    block = errors[4].shape[1]
+    write(
+        4, (all_of, cut(0, block)), every, approx(left[:, 3072:3328], right[:, cut(2816, block)]),
+        mixer_rate,
+    )
 
     @pl.when(step == 0)
     def _():
@@ -1033,7 +1055,7 @@
         grid=(steps,),
         out_shape=[sds(a.shape) for a in matrices] * 3 + [sds(a.shape) for a in vectors] * 2
         + factors + [sds(series.shape)],
-        in_specs=[whole(left), whole(right), whole(mean), VM, VM] + specs * 3 + vector_specs * 2,
+        in_specs=[whole(left), whole(right), whole(mean), VM, VM] + [VM] * 15 + vector_specs * 2,
         out_specs=specs * 3 + vector_specs * 2 + [whole(a) for a in factors] + [HB],
         scratch_shapes=[pltpu.SemaphoreType.DMA((2,))],
         compiler_params=pltpu.CompilerParams(vmem_limit_bytes=LIMITS[7] * MIB),

time: 113 us -> 112 us (level)
  starting transfers between devices: 1.74 us -> 15.8 us
  Pallas kernels: 109 us -> 95.2 us
    ppermute x6, starting transfers between devices: 1.74 us -> 15.8 us  [swap(): return lax.ppermute(values, 'mp', [(0, 1), (1, 0)])]
    pallas_call x4, Pallas kernels: 67 us -> 53 us  [call(): pl.pallas_call(kernel, out_shape=outs, in_specs=in_specs if in_specs is n...]
  transfers between devices with their start and end apart: 6 -> 6, of which waited for: 0 -> 0; matrix products, arithmetic and copies ran while one was open for 0% -> 0% of each run, Pallas kernels for 67% -> 55%
where the time goes in v1:
time: 112 us; the launch traced here: 113 us
  Pallas kernels  95.2 us (85%)
  starting transfers between devices  15.8 us (14%)
  between operations  1.36 us (1%)
    pallas_call x4, Pallas kernels, call(): pl.pallas_call(kernel, out_shape=outs, in_specs=in_specs if in_specs is n...  53 us
    pallas_call x1, Pallas kernels, local(): pl.pallas_call(functools.partial(reduce_factors, replicas), out_shape=[sd...  27 us
    ppermute x6, starting transfers between devices, swap(): return lax.ppermute(values, 'mp', [(0, 1), (1, 0)])  15.8 us
    pallas_call x1, Pallas kernels, local(): pl.pallas_call(functools.partial(renew_all, step_rate, mixer_rate), grid=...  9.58 us
    pallas_call x1, Pallas kernels, local(): pl.pallas_call(prepare, out_shape=[packed, packed, sds((half, history), b...  5.68 us
  transfers between devices with their start and end apart: 6, of which 0 were waited for; matrix products, arithmetic and copies ran while one was open for 0% of the time, Pallas kernels for 55%

profile of v1, /device:TPU:0, one launch (start us, length us, event | category | flops | bytes accessed | tf_op | source)
XLA Modules:
  0.0 112.5 jit_solution(6014832269394973174)
XLA Ops:
  0.7 5.7 %prepare.1 = (bf16[1232,512]{1,0:T(8,128)(2,1)S(1)}, bf16[1232,512]{1,0:T(8,128)(2,1)S(1)}, bf16[448,336]{1,0:T(8,128)(2,1)S(1)}, f32[8,1024]{1,0:T(8,128)S(1)},...) custom-call(s32[2]{0:T(128)} %groups_hbm.1, s32[2]{0:T(128)} %counts_hbm.1, ...), custom_call_target="tpu_custom_call" | custom-call | flops 7000000000 | bytes 14000000 | tf_op jit(solution)/shard_map/prepare/pallas_call | solution.py:930
  6.4 0.5 collective-permute-start
  6.9 10.2 %attend_forward.1 = (f32[896,512]{1,0:T(8,128)S(1)}, bf16[896,512]{1,0:T(8,128)(2,1)S(1)}, bf16[896,512]{1,0:T(8,128)(2,1)S(1)}, bf16[896,512]{1,0:T(8,128)(2,1)...) custom-call(s32[8,128]{1,0:T(8,128)S(1)} %get-tuple-element.118.fact, ...), custom_call_target="tpu_custom_call" | custom-call | flops 15000000512 | bytes 30000000 | tf_op jit(solution)/shard_map/attend_forward/pallas_call | solution.py:882
  17.1 18.2 %feed_forward.1 = (f32[448,512]{1,0:T(8,128)S(1)}, f32[448,512]{1,0:T(8,128)S(1)}, bf16[896,1024]{1,0:T(8,128)(2,1)S(1)}, bf16[896,1024]{1,0:T(8,128)(2,1)S(1)},...) custom-call(s32[8,128]{1,0:T(8,128)S(1)} %get-tuple-element.118.fact, ...), custom_call_target="tpu_custom_call" | custom-call | flops 22000001024 | bytes 44000000 | tf_op jit(solution)/shard_map/feed_forward/pallas_call | solution.py:882
  35.3 14.2 %collective-permute-start.2 = (f32[448,512]{1,0:T(8,128)S(1)}, f32[448,512]{1,0:T(8,128)S(1)}, u32[]{:S(2)}, u32[]{:S(2)}) collective-permute-start(f32[448,512]{1,0:T(8,128)S(1)} %get-tuple-element.135), channel_id=1, source_target_pairs={{0,1},{1,0},{2,3},{3,2},{4,5},{5,4},{6,7},{7,6},{8,9},{9,8},{10,11... | collective-permute-start | bytes 2752520 | tf_op jit(solution)/shard_map/ppermute | solution.py:924
  49.5 0.1 collective-permute-start.1
  49.5 0.0 copy-start.17
  49.6 0.0 copy-start.18
  49.6 21.3 %attend_backward.1 = (f32[3,512,256]{2,1,0:T(8,128)S(1)}, bf16[1104,512]{1,0:T(8,128)(2,1)S(1)}, f32[448,336]{1,0:T(8,128)S(1)}, f32[448,336]{1,0:T(8,128)S(1)},...) custom-call(s32[8,128]{1,0:T(8,128)S(1)} %get-tuple-element.118.facts, bf16[896,512]{1,0:T(8,128)(2,1)S(1)} %get-tuple-element.137.query_ref, ...), custom_call_target="tpu_custom_call" | custom-call | flops 22000001024 | bytes 44000000 | tf_op jit(solution)/shard_map/attend_backward/pallas_call | solution.py:882
  70.8 0.5 collective-permute-start.3
  71.3 0.1 collective-permute-start.4
  71.4 0.4 collective-permute-start.5
  71.9 0.0 copy-start.6
  71.9 0.0 copy-start.19
  72.0 3.4 %feed_matrices.1 = (f32[1024,512]{1,0:T(8,128)S(1)}, f32[512,1024]{1,0:T(8,128)S(1)}, f32[256,512]{1,0:T(8,128)S(1)}, f32[8,1792]{1,0:T(8,128)S(1)}, f32[448,2,512]{2,1,0:T(2,128)}) custom-call(bf16[896,1024]{1,0:T(8,128)(2,1)S(1)} %get-tuple-element.128.active_ref, bf16[896,1024]{1,0:T(8,128)(2,1)S(1)} %get-tuple-element.129.preact_ref, ...), custom_call_target="tpu_custom_call" | custom-call | flops 6000000000 | bytes 12000000 | tf_op jit(solution)/shard_map/feed_matrices/pallas_call | solution.py:882
  75.4 0.0 copy-start.2
  75.5 0.0 copy-start.3
  75.5 0.0 copy-start.8
  75.5 0.0 copy-start.10
  75.5 0.0 copy-start.13
  75.5 0.0 copy-start.14
  75.6 0.0 copy-start.24
  75.6 27.0 %reduce_factors.1 = (f32[8,3328]{1,0:T(8,128)S(1)}, f32[8,3328]{1,0:T(8,128)S(1)}, f32[8,768]{1,0:T(8,128)S(1)}, f32[3,512,256]{2,1,0:T(8,128)S(1)}, f32[3,336,512]{2,1,0:T(8,128)S(1)}) custom-call(s32[8,128]{1,0:T(8,128)S(1)} %get-tuple-element.118.facts, f32[3,512,256]{2,1,0:T(8,128)S(1)} %get-tuple-element.148.near_attend, ...), custom_call_target="tpu_custom_call" | custom-call | flops 30000001024 | bytes 60000000 | tf_op jit(solution)/shard_map/reduce_factors/pallas_call | solution.py:1012
  102.8 9.6 %renew_all.1 = (f32[3,336,512]{2,1,0:T(8,128)}, f32[1024,512]{1,0:T(8,128)}, f32[3,512,256]{2,1,0:T(8,128)}, f32[512,1024]{1,0:T(8,128)}, f32[256,512]{1,0:T(8,1...) custom-call(f32[8,3328]{1,0:T(8,128)S(1)} %get-tuple-element.156.lef, ...), custom_call_target="tpu_custom_call" | custom-call | flops 12000000000 | bytes 24000000 | tf_op jit(solution)/shard_map/renew_all/pallas_call | solution.py:1053
  (55 shorter events, 0.1 us)
Async XLA Ops:
  6.4 10.7 %collective-permute-start = (bf16[2752,512]{1,0:T(8,128)(2,1)S(1)}, bf16[2752,512]{1,0:T(8,128)(2,1)S(1)}, u32[]{:S(2)}, u32[]{:S(2)}) collective-permute-start(bf16[2752,512]{1,0:T(8,128)(2,1)S(1)} %get-tuple-element.125.own), channel_id=1, source_target_pairs={{0,1},{1,0},{2,3},{3,2},{4,5},{5,4},{6,7},{7,6},{8,9},{9,8},{10,11... | collective-permute-start | bytes 8454152 | tf_op jit(solution)/shard_map/ppermute | solution.py:924
  35.3 36.6 %collective-permute-start.2 = (f32[448,512]{1,0:T(8,128)S(1)}, f32[448,512]{1,0:T(8,128)S(1)}, u32[]{:S(2)}, u32[]{:S(2)}) collective-permute-start(f32[448,512]{1,0:T(8,128)S(1)} %get-tuple-element.135), channel_id=1, source_target_pairs={{0,1},{1,0},{2,3},{3,2},{4,5},{5,4},{6,7},{7,6},{8,9},{9,8},{10,11... | collective-permute-start | bytes 2752520 | tf_op jit(solution)/shard_map/ppermute | solution.py:924
  49.5 22.4 %collective-permute-start.1 = (bf16[2304,512]{1,0:T(8,128)(2,1)S(1)}, bf16[2304,512]{1,0:T(8,128)(2,1)S(1)}, u32[]{:S(2)}, u32[]{:S(2)}) collective-permute-start(bf16[2304,512]{1,0:T(8,128)(2,1)S(1)} %get-tuple-element.133), channel_id=1, source_target_pairs={{0,1},{1,0},{2,3},{3,2},{4,5},{5,4},{6,7},{7,6},{8,9},{9,8},{10,11... | collective-permute-start | bytes 7077896 | tf_op jit(solution)/shard_map/ppermute | solution.py:924
  49.5 22.4 %copy-start.17 = (f32[1,512,8]{1,2,0:T(8,128)S(1)}, f32[1,512,8]{1,2,0:T(8,128)}, u32[]{:S(2)}) copy-start(f32[1,512,8]{1,2,0:T(8,128)} %param.57) | copy-start | bytes 49156
  49.6 22.4 %copy-start.18 = (f32[1,512,8]{1,2,0:T(8,128)S(1)}, f32[1,512,8]{1,2,0:T(8,128)}, u32[]{:S(2)}) copy-start(f32[1,512,8]{1,2,0:T(8,128)} %param.49) | copy-start | bytes 49156
  70.8 4.6 %collective-permute-start.3 = (bf16[1104,512]{1,0:T(8,128)(2,1)S(1)}, bf16[1104,512]{1,0:T(8,128)(2,1)S(1)}, u32[]{:S(2)}, u32[]{:S(2)}) collective-permute-start(bf16[1104,512]{1,0:T(8,128)(2,1)S(1)} %get-tuple-element.149.own), channel_id=1, source_target_pairs={{0,1},{1,0},{2,3},{3,2},{4,5},{5,4},{6,7},{7,6},{8,9},{9,8},{10,11... | collective-permute-start | bytes 3391496 | tf_op jit(solution)/shard_map/ppermute | solution.py:924
  71.3 4.0 %collective-permute-start.4 = (f32[16,512]{1,0:T(8,128)S(1)}, f32[16,512]{1,0:T(8,128)S(1)}, u32[]{:S(2)}, u32[]{:S(2)}) collective-permute-start(f32[16,512]{1,0:T(8,128)S(1)} %get-tuple-element.152), channel_id=1, source_target_pairs={{0,1},{1,0},{2,3},{3,2},{4,5},{5,4},{6,7},{7,6},{8,9},{9,8},{10,11... | collective-permute-start | bytes 98312 | tf_op jit(solution)/shard_map/ppermute | solution.py:924
  71.4 31.2 %collective-permute-start.5 = (f32[448,336]{1,0:T(8,128)S(1)}, f32[448,336]{1,0:T(8,128)S(1)}, u32[]{:S(2)}, u32[]{:S(2)}) collective-permute-start(f32[448,336]{1,0:T(8,128)S(1)} %get-tuple-element.160), channel_id=1, source_target_pairs={{0,1},{1,0},{2,3},{3,2},{4,5},{5,4},{6,7},{7,6},{8,9},{9,8},{10,11... | collective-permute-start | bytes 1806344 | tf_op jit(solution)/shard_map/ppermute | solution.py:924
  75.4 27.2 %copy-start.2 = (f32[512,1024]{1,0:T(8,128)S(1)}, f32[512,1024]{1,0:T(8,128)}, u32[]{:S(2)}) copy-start(f32[512,1024]{1,0:T(8,128)} %refs_8_.1) | copy-start | bytes 6291460
  75.5 27.2 %copy-start.3 = (f32[1024,512]{1,0:T(8,128)S(1)}, f32[1024,512]{1,0:T(8,128)}, u32[]{:S(2)}) copy-start(f32[1024,512]{1,0:T(8,128)} %refs_6_.1) | copy-start | bytes 6291460
  75.5 27.2 %copy-start.4 = (f32[1024,512]{1,0:T(8,128)S(1)}, f32[1024,512]{1,0:T(8,128)}, u32[]{:S(2)}) copy-start(f32[1024,512]{1,0:T(8,128)} %refs_11_.1) | copy-start | bytes 6291460
  75.5 27.2 %copy-start.5 = (f32[512,1024]{1,0:T(8,128)S(1)}, f32[512,1024]{1,0:T(8,128)}, u32[]{:S(2)}) copy-start(f32[512,1024]{1,0:T(8,128)} %refs_13_.1) | copy-start | bytes 6291460
  75.5 27.2 %copy-start.8 = (f32[3,336,512]{2,1,0:T(8,128)S(1)}, f32[3,336,512]{2,1,0:T(8,128)}, u32[]{:S(2)}) copy-start(f32[3,336,512]{2,1,0:T(8,128)} %refs_10_.1) | copy-start | bytes 6193156
  75.5 27.2 %copy-start.10 = (f32[512,3,256]{2,0,1:T(8,128)S(1)}, f32[512,3,256]{2,0,1:T(8,128)}, u32[]{:S(2)}) copy-start(f32[512,3,256]{2,0,1:T(8,128)} %param.42) | copy-start | bytes 4718596
  75.5 27.2 %copy-start.11 = (f32[512,3,256]{2,0,1:T(8,128)S(1)}, f32[512,3,256]{2,0,1:T(8,128)}, u32[]{:S(2)}) copy-start(f32[512,3,256]{2,0,1:T(8,128)} %param.43) | copy-start | bytes 4718596
  75.5 27.2 %copy-start.13 = (f32[256,512]{1,0:T(8,128)S(1)}, f32[256,512]{1,0:T(8,128)}, u32[]{:S(2)}) copy-start(f32[256,512]{1,0:T(8,128)} %refs_9_.1) | copy-start | bytes 1572868
  75.5 27.2 %copy-start.14 = (f32[256,512]{1,0:T(8,128)S(1)}, f32[256,512]{1,0:T(8,128)}, u32[]{:S(2)}) copy-start(f32[256,512]{1,0:T(8,128)} %refs_14_.1) | copy-start | bytes 1572868
  75.5 27.2 %copy-start.22 = (f32[3,512]{1,0:T(4,128)S(1)}, f32[3,512]{1,0:T(4,128)}, u32[]{:S(2)}) copy-start(f32[3,512]{1,0:T(4,128)} %refs_20_.1) | copy-start | bytes 18436
  75.6 27.2 %copy-start.23 = (f32[4,512]{1,0:T(4,128)S(1)}, f32[4,512]{1,0:T(4,128)}, u32[]{:S(2)}) copy-start(f32[4,512]{1,0:T(4,128)} %refs_22_.1) | copy-start | bytes 24580
  75.6 27.2 %copy-start.24 = (f32[1024]{0:T(1024)S(1)}, f32[1024]{0:T(1024)}, u32[]{:S(2)}) copy-start(f32[1024]{0:T(1024)} %param.62) | copy-start | bytes 12292
  75.6 27.2 %copy-start.26 = (f32[2,512]{1,0:T(2,128)S(1)}, f32[2,512]{1,0:T(2,128)}, u32[]{:S(2)}) copy-start(f32[2,512]{1,0:T(2,128)} %refs_21_.1) | copy-start | bytes 12292
  75.6 27.2 %copy-start.27 = (f32[1024]{0:T(1024)S(1)}, f32[1024]{0:T(1024)}, u32[]{:S(2)}) copy-start(f32[1024]{0:T(1024)} %param.63) | copy-start | bytes 12292
  75.6 27.2 %copy-start.28 = (f32[2,256]{1,0:T(2,128)S(1)}, f32[2,256]{1,0:T(2,128)}, u32[]{:S(2)}) copy-start(f32[2,256]{1,0:T(2,128)} %refs_18_.1) | copy-start | bytes 6148
  75.6 27.1 %copy-start.29 = (f32[2,256]{1,0:T(2,128)S(1)}, f32[2,256]{1,0:T(2,128)}, u32[]{:S(2)}) copy-start(f32[2,256]{1,0:T(2,128)} %refs_23_.1) | copy-start | bytes 6148
  (12 other events, 136.1 us)

commit v2 on v1

--- a/solution.py
+++ b/solution.py
@@ -279,7 +279,8 @@
     extra_query = jnp.where(
         last, 1.0, dot_tn(jnp.concatenate(three_parts(peak_ref[...]), axis=0), spread)
     ).astype(bf16)
-    extra_key = jnp.where(last & dead, -1e30, 0.0)
+    extra_key = jnp.where(last & dead, -1e30, 0.0).astype(bf16)
+    unit = jnp.ones((rows, 128), bf16)
 
     def pair(index, carry):
         columns = pl.ds(pl.multiple_of(index * 128, 128), 128)
@@ -291,7 +292,7 @@
             mine = (lane >= head_dim) if side else (lane < head_dim)
             hot = lax.rem(lane, 64) // 3 == index * 2 + side
             scores = dot_nt(
-                jnp.where(mine, keys, jnp.where(hot, 1.0, extra_key).astype(bf16)),
+                jnp.where(mine, keys, jnp.where(hot, unit, extra_key)),
                 jnp.where(mine, queries, extra_query),
             )
             soft = jnp.exp2(scores).astype(bf16)
@@ -492,7 +493,8 @@
     extra_query = jnp.where(
         last, 1.0, dot_tn(jnp.concatenate(three_parts(lse_ref[...]), axis=0), spread)
     ).astype(bf16)
-    extra_key = jnp.where(last & dead, -1e30, 0.0)
+    extra_key = jnp.where(last & dead, -1e30, 0.0).astype(bf16)
+    unit = jnp.ones((rows, 128), bf16)
     extra_grad = delta_ref[...]
     nothing = jnp.zeros((rows, 128), bf16)
 
@@ -508,12 +510,12 @@
             hot = lax.rem(lane, 64) // 3 == index * 2 + side
             soft = jnp.exp2(
                 dot_nt(
-                    jnp.where(mine, keys, jnp.where(hot, 1.0, extra_key).astype(bf16)),
+                    jnp.where(mine, keys, jnp.where(hot, unit, extra_key)),
                     jnp.where(mine, queries, extra_query),
                 )
             )
             centered = dot_nt(
-                jnp.where(mine, values, jnp.where(hot, 1.0, 0.0).astype(bf16)),
+                jnp.where(mine, values, jnp.where(hot, unit, nothing)),
                 jnp.where(mine, grads, extra_grad),
             )
             softs.append(soft.astype(bf16))

time: 112 us -> 112 us (level)
  starting transfers between devices: 15.8 us -> 1.75 us
  Pallas kernels: 95.2 us -> 109 us
    ppermute x6, starting transfers between devices: 15.8 us -> 1.75 us  [swap(): return lax.ppermute(values, 'mp', [(0, 1), (1, 0)])]
    pallas_call x1, Pallas kernels: 27 us -> 40.6 us  [local(): pl.pallas_call(functools.partial(reduce_factors, replicas), out_shape=[sd...]
  transfers between devices with their start and end apart: 6 -> 6, of which waited for: 0 -> 0; matrix products, arithmetic and copies ran while one was open for 0% -> 0% of each run, Pallas kernels for 55% -> 67%
where the time goes in v2:
time: 112 us
  Pallas kernels  109 us (97%)
  starting transfers between devices  1.75 us (2%)
  between operations  1.36 us (1%)
    pallas_call x4, Pallas kernels, call(): pl.pallas_call(kernel, out_shape=outs, in_specs=in_specs if in_specs is n...  52.9 us
    pallas_call x1, Pallas kernels, local(): pl.pallas_call(functools.partial(reduce_factors, replicas), out_shape=[sd...  40.6 us
    pallas_call x1, Pallas kernels, local(): pl.pallas_call(functools.partial(renew_all, step_rate, mixer_rate), grid=...  9.57 us
    pallas_call x1, Pallas kernels, local(): pl.pallas_call(prepare, out_shape=[packed, packed, sds((half, history), b...  5.68 us
  transfers between devices with their start and end apart: 6, of which 0 were waited for; matrix products, arithmetic and copies ran while one was open for 0% of the time, Pallas kernels for 67%

profile of v2, /device:TPU:0, one launch (start us, length us, event | category | flops | bytes accessed | tf_op | source)
XLA Modules:
  0.0 112.1 jit_solution(17640218068808353159)
XLA Ops:
  0.7 5.7 %prepare.1 = (bf16[1232,512]{1,0:T(8,128)(2,1)S(1)}, bf16[1232,512]{1,0:T(8,128)(2,1)S(1)}, bf16[448,336]{1,0:T(8,128)(2,1)S(1)}, f32[8,1024]{1,0:T(8,128)S(1)},...) custom-call(s32[2]{0:T(128)} %groups_hbm.1, s32[2]{0:T(128)} %counts_hbm.1, ...), custom_call_target="tpu_custom_call" | custom-call | flops 7000000000 | bytes 14000000 | tf_op jit(solution)/shard_map/prepare/pallas_call | solution.py:932
  6.4 0.5 collective-permute-start
  6.9 10.1 %attend_forward.1 = (f32[896,512]{1,0:T(8,128)S(1)}, bf16[896,512]{1,0:T(8,128)(2,1)S(1)}, bf16[896,512]{1,0:T(8,128)(2,1)S(1)}, bf16[896,512]{1,0:T(8,128)(2,1)...) custom-call(s32[8,128]{1,0:T(8,128)S(1)} %get-tuple-element.118.fact, ...), custom_call_target="tpu_custom_call" | custom-call | flops 15000000512 | bytes 30000000 | tf_op jit(solution)/shard_map/attend_forward/pallas_call | solution.py:884
  17.0 18.2 %feed_forward.1 = (f32[448,512]{1,0:T(8,128)S(1)}, f32[448,512]{1,0:T(8,128)S(1)}, bf16[896,1024]{1,0:T(8,128)(2,1)S(1)}, bf16[896,1024]{1,0:T(8,128)(2,1)S(1)},...) custom-call(s32[8,128]{1,0:T(8,128)S(1)} %get-tuple-element.118.fact, ...), custom_call_target="tpu_custom_call" | custom-call | flops 22000001024 | bytes 44000000 | tf_op jit(solution)/shard_map/feed_forward/pallas_call | solution.py:884
  35.2 0.1 collective-permute-start.2
  35.3 0.5 collective-permute-start.1
  35.8 0.0 copy-start.17
  35.8 0.0 copy-start.18
  35.8 21.2 %attend_backward.1 = (f32[3,512,256]{2,1,0:T(8,128)S(1)}, bf16[1104,512]{1,0:T(8,128)(2,1)S(1)}, f32[448,336]{1,0:T(8,128)S(1)}, f32[448,336]{1,0:T(8,128)S(1)},...) custom-call(s32[8,128]{1,0:T(8,128)S(1)} %get-tuple-element.118.facts, bf16[896,512]{1,0:T(8,128)(2,1)S(1)} %get-tuple-element.137.query_ref, ...), custom_call_target="tpu_custom_call" | custom-call | flops 22000001024 | bytes 44000000 | tf_op jit(solution)/shard_map/attend_backward/pallas_call | solution.py:884
  57.1 0.1 collective-permute-start.3
  57.2 0.4 collective-permute-start.4
  57.7 0.1 collective-permute-start.5
  57.8 0.0 copy-start.6
  57.8 0.0 copy-start.9
  57.9 3.4 %feed_matrices.1 = (f32[1024,512]{1,0:T(8,128)S(1)}, f32[512,1024]{1,0:T(8,128)S(1)}, f32[256,512]{1,0:T(8,128)S(1)}, f32[8,1792]{1,0:T(8,128)S(1)}, f32[448,2,512]{2,1,0:T(2,128)}) custom-call(bf16[896,1024]{1,0:T(8,128)(2,1)S(1)} %get-tuple-element.128.active_ref, bf16[896,1024]{1,0:T(8,128)(2,1)S(1)} %get-tuple-element.129.preact_ref, ...), custom_call_target="tpu_custom_call" | custom-call | flops 6000000000 | bytes 12000000 | tf_op jit(solution)/shard_map/feed_matrices/pallas_call | solution.py:884
  61.3 0.0 copy-start.3
  61.4 0.0 copy-start.4
  61.4 0.0 copy-start.10
  61.4 0.0 copy-start.11
  61.4 0.0 copy-start.22
  61.5 0.0 copy-start.23
  61.5 0.0 copy-start.26
  61.5 40.6 %reduce_factors.1 = (f32[8,3328]{1,0:T(8,128)S(1)}, f32[8,3328]{1,0:T(8,128)S(1)}, f32[8,768]{1,0:T(8,128)S(1)}, f32[3,512,256]{2,1,0:T(8,128)S(1)}, f32[3,336,512]{2,1,0:T(8,128)S(1)}) custom-call(s32[8,128]{1,0:T(8,128)S(1)} %get-tuple-element.118.facts, f32[3,512,256]{2,1,0:T(8,128)S(1)} %get-tuple-element.148.near_attend, ...), custom_call_target="tpu_custom_call" | custom-call | flops 30000001024 | bytes 60000000 | tf_op jit(solution)/shard_map/reduce_factors/pallas_call | solution.py:1014
  102.3 9.6 %renew_all.1 = (f32[3,336,512]{2,1,0:T(8,128)}, f32[1024,512]{1,0:T(8,128)}, f32[3,512,256]{2,1,0:T(8,128)}, f32[512,1024]{1,0:T(8,128)}, f32[256,512]{1,0:T(8,1...) custom-call(f32[8,3328]{1,0:T(8,128)S(1)} %get-tuple-element.156.lef, ...), custom_call_target="tpu_custom_call" | custom-call | flops 12000000000 | bytes 24000000 | tf_op jit(solution)/shard_map/renew_all/pallas_call | solution.py:1055
  (55 shorter events, 0.1 us)
Async XLA Ops:
  6.4 10.6 %collective-permute-start = (bf16[2752,512]{1,0:T(8,128)(2,1)S(1)}, bf16[2752,512]{1,0:T(8,128)(2,1)S(1)}, u32[]{:S(2)}, u32[]{:S(2)}) collective-permute-start(bf16[2752,512]{1,0:T(8,128)(2,1)S(1)} %get-tuple-element.125.own), channel_id=1, source_target_pairs={{0,1},{1,0},{2,3},{3,2},{4,5},{5,4},{6,7},{7,6},{8,9},{9,8},{10,11... | collective-permute-start | bytes 8454152 | tf_op jit(solution)/shard_map/ppermute | solution.py:926
  35.2 22.5 %collective-permute-start.2 = (f32[448,512]{1,0:T(8,128)S(1)}, f32[448,512]{1,0:T(8,128)S(1)}, u32[]{:S(2)}, u32[]{:S(2)}) collective-permute-start(f32[448,512]{1,0:T(8,128)S(1)} %get-tuple-element.135), channel_id=1, source_target_pairs={{0,1},{1,0},{2,3},{3,2},{4,5},{5,4},{6,7},{7,6},{8,9},{9,8},{10,11... | collective-permute-start | bytes 2752520 | tf_op jit(solution)/shard_map/ppermute | solution.py:926
  35.3 22.4 %collective-permute-start.1 = (bf16[2304,512]{1,0:T(8,128)(2,1)S(1)}, bf16[2304,512]{1,0:T(8,128)(2,1)S(1)}, u32[]{:S(2)}, u32[]{:S(2)}) collective-permute-start(bf16[2304,512]{1,0:T(8,128)(2,1)S(1)} %get-tuple-element.133), channel_id=1, source_target_pairs={{0,1},{1,0},{2,3},{3,2},{4,5},{5,4},{6,7},{7,6},{8,9},{9,8},{10,11... | collective-permute-start | bytes 7077896 | tf_op jit(solution)/shard_map/ppermute | solution.py:926
  35.8 22.0 %copy-start.17 = (f32[1,512,8]{1,2,0:T(8,128)S(1)}, f32[1,512,8]{1,2,0:T(8,128)}, u32[]{:S(2)}) copy-start(f32[1,512,8]{1,2,0:T(8,128)} %param.57) | copy-start | bytes 49156
  35.8 22.0 %copy-start.18 = (f32[1,512,8]{1,2,0:T(8,128)S(1)}, f32[1,512,8]{1,2,0:T(8,128)}, u32[]{:S(2)}) copy-start(f32[1,512,8]{1,2,0:T(8,128)} %param.49) | copy-start | bytes 49156
  57.1 4.2 %collective-permute-start.3 = (bf16[1104,512]{1,0:T(8,128)(2,1)S(1)}, bf16[1104,512]{1,0:T(8,128)(2,1)S(1)}, u32[]{:S(2)}, u32[]{:S(2)}) collective-permute-start(bf16[1104,512]{1,0:T(8,128)(2,1)S(1)} %get-tuple-element.149.own), channel_id=1, source_target_pairs={{0,1},{1,0},{2,3},{3,2},{4,5},{5,4},{6,7},{7,6},{8,9},{9,8},{10,11... | collective-permute-start | bytes 3391496 | tf_op jit(solution)/shard_map/ppermute | solution.py:926
  57.2 4.0 %collective-permute-start.4 = (f32[16,512]{1,0:T(8,128)S(1)}, f32[16,512]{1,0:T(8,128)S(1)}, u32[]{:S(2)}, u32[]{:S(2)}) collective-permute-start(f32[16,512]{1,0:T(8,128)S(1)} %get-tuple-element.152), channel_id=1, source_target_pairs={{0,1},{1,0},{2,3},{3,2},{4,5},{5,4},{6,7},{7,6},{8,9},{9,8},{10,11... | collective-permute-start | bytes 98312 | tf_op jit(solution)/shard_map/ppermute | solution.py:926
  57.7 44.5 %collective-permute-start.5 = (f32[448,336]{1,0:T(8,128)S(1)}, f32[448,336]{1,0:T(8,128)S(1)}, u32[]{:S(2)}, u32[]{:S(2)}) collective-permute-start(f32[448,336]{1,0:T(8,128)S(1)} %get-tuple-element.160), channel_id=1, source_target_pairs={{0,1},{1,0},{2,3},{3,2},{4,5},{5,4},{6,7},{7,6},{8,9},{9,8},{10,11... | collective-permute-start | bytes 1806344 | tf_op jit(solution)/shard_map/ppermute | solution.py:926
  61.3 40.8 %copy-start.2 = (f32[512,1024]{1,0:T(8,128)S(1)}, f32[512,1024]{1,0:T(8,128)}, u32[]{:S(2)}) copy-start(f32[512,1024]{1,0:T(8,128)} %refs_8_.1) | copy-start | bytes 6291460
  61.3 40.8 %copy-start.3 = (f32[1024,512]{1,0:T(8,128)S(1)}, f32[1024,512]{1,0:T(8,128)}, u32[]{:S(2)}) copy-start(f32[1024,512]{1,0:T(8,128)} %refs_6_.1) | copy-start | bytes 6291460
  61.4 40.8 %copy-start.4 = (f32[1024,512]{1,0:T(8,128)S(1)}, f32[1024,512]{1,0:T(8,128)}, u32[]{:S(2)}) copy-start(f32[1024,512]{1,0:T(8,128)} %refs_11_.1) | copy-start | bytes 6291460
  61.4 40.8 %copy-start.5 = (f32[512,1024]{1,0:T(8,128)S(1)}, f32[512,1024]{1,0:T(8,128)}, u32[]{:S(2)}) copy-start(f32[512,1024]{1,0:T(8,128)} %refs_13_.1) | copy-start | bytes 6291460
  61.4 40.8 %copy-start.8 = (f32[3,336,512]{2,1,0:T(8,128)S(1)}, f32[3,336,512]{2,1,0:T(8,128)}, u32[]{:S(2)}) copy-start(f32[3,336,512]{2,1,0:T(8,128)} %refs_10_.1) | copy-start | bytes 6193156
  61.4 40.8 %copy-start.10 = (f32[512,3,256]{2,0,1:T(8,128)S(1)}, f32[512,3,256]{2,0,1:T(8,128)}, u32[]{:S(2)}) copy-start(f32[512,3,256]{2,0,1:T(8,128)} %param.42) | copy-start | bytes 4718596
  61.4 40.8 %copy-start.11 = (f32[512,3,256]{2,0,1:T(8,128)S(1)}, f32[512,3,256]{2,0,1:T(8,128)}, u32[]{:S(2)}) copy-start(f32[512,3,256]{2,0,1:T(8,128)} %param.43) | copy-start | bytes 4718596
  61.4 40.8 %copy-start.13 = (f32[256,512]{1,0:T(8,128)S(1)}, f32[256,512]{1,0:T(8,128)}, u32[]{:S(2)}) copy-start(f32[256,512]{1,0:T(8,128)} %refs_9_.1) | copy-start | bytes 1572868
  61.4 40.8 %copy-start.14 = (f32[256,512]{1,0:T(8,128)S(1)}, f32[256,512]{1,0:T(8,128)}, u32[]{:S(2)}) copy-start(f32[256,512]{1,0:T(8,128)} %refs_14_.1) | copy-start | bytes 1572868
  61.4 40.8 %copy-start.22 = (f32[3,512]{1,0:T(4,128)S(1)}, f32[3,512]{1,0:T(4,128)}, u32[]{:S(2)}) copy-start(f32[3,512]{1,0:T(4,128)} %refs_20_.1) | copy-start | bytes 18436
  61.5 40.8 %copy-start.23 = (f32[4,512]{1,0:T(4,128)S(1)}, f32[4,512]{1,0:T(4,128)}, u32[]{:S(2)}) copy-start(f32[4,512]{1,0:T(4,128)} %refs_22_.1) | copy-start | bytes 24580
  61.5 40.8 %copy-start.24 = (f32[1024]{0:T(1024)S(1)}, f32[1024]{0:T(1024)}, u32[]{:S(2)}) copy-start(f32[1024]{0:T(1024)} %param.62) | copy-start | bytes 12292
  61.5 40.8 %copy-start.26 = (f32[2,512]{1,0:T(2,128)S(1)}, f32[2,512]{1,0:T(2,128)}, u32[]{:S(2)}) copy-start(f32[2,512]{1,0:T(2,128)} %refs_21_.1) | copy-start | bytes 12292
  61.5 40.8 %copy-start.27 = (f32[1024]{0:T(1024)S(1)}, f32[1024]{0:T(1024)}, u32[]{:S(2)}) copy-start(f32[1024]{0:T(1024)} %param.63) | copy-start | bytes 12292
  61.5 40.8 %copy-start.28 = (f32[2,256]{1,0:T(2,128)S(1)}, f32[2,256]{1,0:T(2,128)}, u32[]{:S(2)}) copy-start(f32[2,256]{1,0:T(2,128)} %refs_18_.1) | copy-start | bytes 6148
  61.5 40.8 %copy-start.29 = (f32[2,256]{1,0:T(2,128)S(1)}, f32[2,256]{1,0:T(2,128)}, u32[]{:S(2)}) copy-start(f32[2,256]{1,0:T(2,128)} %refs_23_.1) | copy-start | bytes 6148
  (12 other events, 134.5 us)
